TPU v7x, 32 devices: a whole 2x2x4 slice. The times are simulated.
32 devices in a mesh: groups: 2 (over x), cell: 16 (over z, y, core).
Axes of the slice: x: 2, y: 2, z: 4, core: 2. Of those that a mesh axis runs over, the one named last changes fastest.
Arguments:
- positions: float32 [3, 196608], P(None, ('groups', 'cell')), parts along dimension 1, may hold values from -1 to 1
- deltas: float32 [196608], P(('groups', 'cell')), parts along dimension 0, may hold values from 0.02 to 0.1
- background: float32 [3, 2048], P(None, ('groups', 'cell')), parts along dimension 1, may hold values from 0 to 1
- target: float32 [3, 2048], P(None, ('groups', 'cell')), parts along dimension 1, may hold values from 0 to 1
- ray_codes: int32 [2048], P(('groups', 'cell')), parts along dimension 0, may hold values from 0 to 2047
- frequencies: float32 [3, 64], replicated, may hold values from -16 to 16
- w_first: bfloat16 [32, 128, 256], P('cell'), may hold values from -0.5 to 0.5
- b_first: float32 [32, 256], P('cell'), may hold values from -3 to 3
- w_second: bfloat16 [32, 256, 256], P('cell'), may hold values from -0.375 to 0.375
- b_second: float32 [32, 256], P('cell'), may hold values from -3 to 3
- head_out: bfloat16 [32, 4, 256], P('cell'), may hold values from -0.375 to 0.375
- head_app: bfloat16 [32, 3, 48], P('cell'), may hold values from -0.875 to 0.875
- app_table: float32 [48, 2048], replicated, may hold values from -5 to 5
- dispatch: int32 [1024, 192], P(('groups', 'cell')), parts along dimension 0, may hold values from 0 to 6143, as said below
- counts: int32 [1024], P(('groups', 'cell')), parts along dimension 0, may hold values from 0 to 192, as said below
Outputs:
- grad_w_first: float32 [64, 128, 256], P(('groups', 'cell')), parts along dimension 0
- grad_b_first: float32 [64, 256], P(('groups', 'cell')), parts along dimension 0
- grad_w_second: float32 [64, 256, 256], P(('groups', 'cell')), parts along dimension 0
- grad_b_second: float32 [64, 256], P(('groups', 'cell')), parts along dimension 0
- grad_head_out: float32 [64, 4, 256], P(('groups', 'cell')), parts along dimension 0
- grad_head_app: float32 [64, 3, 48], P(('groups', 'cell')), parts along dimension 0
- grad_table: float32 [96, 2048], P('groups'), parts along dimension 0
There are 2 independent parts, one for each index of `groups`. A program takes and returns all parts, laid end to end along the dimension named above; an argument that names none is the same for every part. Nothing has to cross between parts.
Inputs may be any that keep to these rules, and one draw needn't show every extreme that they name: `dispatch`: on each device the 32 x 192 entries are a permutation of its rows 0 to 6143; a row lies in cell c when it stands among the first counts entries of c's list, and in no cell otherwise. `counts`: one cell has 192 samples on every device.
All inputs are finite; a program needn't handle non-finite values.
Results may differ from a plain program's by a relative error of at most 0.0058.
Values may be sent and summed in bfloat16 or wider, within the bound.
A program may use at most 128 MiB of HBM per device.

v0:
```python
import jax
import jax.numpy as jnp
from jax import lax
from jax.sharding import PartitionSpec as P

loss_scale = 256.0


def encode(coord_x, coord_y, coord_z, frequencies):
    angle_arg = coord_x[..., None] * frequencies[0] + coord_y[..., None] * frequencies[1]
    angle_arg = angle_arg + coord_z[..., None] * frequencies[2]
    return jnp.concatenate([jnp.sin(angle_arg), jnp.cos(angle_arg)], axis=-1).astype(jnp.bfloat16)


def silu_slope(pre_value):
    sigmoid_value = jax.nn.sigmoid(pre_value)
    return sigmoid_value * (1.0 + pre_value * (1.0 - sigmoid_value))


def composite_loss(raw_values, routed, deltas, background, target):
    density = routed * jax.nn.softplus(raw_values[..., 0])
    optical = density * deltas
    running = jnp.cumsum(optical, axis=1)
    before = jnp.concatenate([jnp.zeros_like(optical[:, :1]), running[:, :-1]], axis=1)
    weight = jnp.exp(-before) * (1.0 - jnp.exp(-optical))
    colors = jax.nn.sigmoid(raw_values[..., 1:4])
    pixels = (
        jnp.einsum("rs,rsk->kr", weight, colors) + jnp.exp(-running[:, -1])[None, :] * background
    )
    return loss_scale * 0.5 * jnp.sum((pixels - target) ** 2)


def code_table(code_ids, cell_index, codes_total):
    flat_ids = code_ids[:, cell_index, :].reshape(-1)
    return (flat_ids[:, None] == jnp.arange(codes_total, dtype=jnp.int32)[None, :]).astype(
        jnp.bfloat16
    )


def lookup_codes(code_ids, projected):
    cell_dev = projected.shape[0]
    codes_total = projected.shape[1]

    def one_cell(cell_index):
        table = code_table(code_ids, cell_index, codes_total)
        return jnp.dot(
            table,
            projected[cell_index],
            precision=lax.Precision.HIGHEST,
            preferred_element_type=jnp.float32,
        )

    picked = lax.map(one_cell, jnp.arange(cell_dev, dtype=jnp.int32))
    picked = picked.reshape(cell_dev, code_ids.shape[0], code_ids.shape[2], 3)
    return jnp.transpose(picked, (1, 0, 2, 3))


def owner_forward(encoded, code_ids, w_first, b_first, w_second, b_second, head_out, projected):
    pre_first = (
        jnp.einsum("njse,jew->njsw", encoded, w_first, preferred_element_type=jnp.float32)
        + b_first[None, :, None, :]
    )
    act_first = jax.nn.silu(pre_first).astype(jnp.bfloat16)
    pre_second = (
        jnp.einsum("njsw,jwv->njsv", act_first, w_second, preferred_element_type=jnp.float32)
        + b_second[None, :, None, :]
    )
    act_second = jax.nn.silu(pre_second).astype(jnp.bfloat16)
    outputs = jnp.einsum("njsw,jow->njso", act_second, head_out, preferred_element_type=jnp.float32)
    appear = lookup_codes(code_ids, projected)
    color_shift = jnp.concatenate(
        [jnp.zeros(appear.shape[:-1] + (1,), jnp.float32), appear], axis=-1
    )
    raw_values = (outputs + color_shift).astype(jnp.bfloat16)
    return (raw_values, pre_first, act_first, pre_second, act_second)


def local(
    positions,
    deltas,
    background,
    target,
    ray_codes,
    frequencies,
    w_first,
    b_first,
    w_second,
    b_second,
    head_out,
    head_app,
    app_table,
    dispatch,
    counts,
):
    cell_axis_size = lax.axis_size("cell")
    capacity = dispatch.shape[1]
    cell_dev = w_first.shape[0]
    rows_local = positions.shape[1]
    rays_local = ray_codes.shape[0]
    samples = rows_local // rays_local
    codes_total = app_table.shape[1]
    listed = dispatch.reshape(-1)
    inverse = (
        jnp.zeros((rows_local,), jnp.int32).at[listed].set(jnp.arange(rows_local, dtype=jnp.int32))
    )
    slot_codes = ray_codes[listed // samples].reshape(cell_axis_size, cell_dev, capacity)
    live_mask = (jnp.arange(capacity, dtype=jnp.int32)[None, :] < counts[:, None]).astype(
        jnp.float32
    )
    routed = live_mask.reshape(-1)[inverse]
    projected = jnp.einsum(
        "jka,ac->jck", head_app.astype(jnp.float32), app_table, precision=lax.Precision.HIGHEST
    )
    slot_positions = positions[:, listed]
    slot_encoded = encode(slot_positions[0], slot_positions[1], slot_positions[2], frequencies)
    slot_features = slot_encoded.reshape(cell_axis_size, cell_dev, capacity, slot_encoded.shape[1])
    encoded = lax.all_to_all(slot_features, "cell", split_axis=0, concat_axis=0, tiled=True)
    finish_code_ids = lax.all_to_all(slot_codes, "cell", split_axis=0, concat_axis=0, tiled=True)
    produced = owner_forward(
        encoded, finish_code_ids, w_first, b_first, w_second, b_second, head_out, projected
    )
    kept_parts = (encoded, finish_code_ids) + produced
    encoded = kept_parts[0]
    code_ids = kept_parts[1]
    raw_back = lax.all_to_all(kept_parts[2], "cell", split_axis=0, concat_axis=0, tiled=True)
    raw_columns = raw_back.reshape(-1, 4).T[:, inverse]
    raw_rows = raw_columns.T
    slope_rows = jax.grad(composite_loss)(
        raw_rows.astype(jnp.float32).reshape(rays_local, samples, 4),
        routed.reshape(rays_local, samples),
        deltas.reshape(rays_local, samples),
        background,
        target,
    )
    slope_columns = slope_rows.reshape(rows_local, 4).astype(jnp.bfloat16).T[:, listed]
    slope_slots = slope_columns.T.reshape(cell_axis_size, cell_dev, capacity, 4)
    slopes = lax.all_to_all(slope_slots, "cell", split_axis=0, concat_axis=0, tiled=True)
    pre_first, act_first, pre_second, act_second = (
        kept_parts[3],
        kept_parts[4],
        kept_parts[5],
        kept_parts[6],
    )
    grad_head_out = jnp.einsum(
        "njso,njsw->jow", slopes, act_second, preferred_element_type=jnp.float32
    )
    back_second = jnp.einsum("njso,jow->njsw", slopes, head_out, preferred_element_type=jnp.float32)
    delta_second = (back_second * silu_slope(pre_second)).astype(jnp.bfloat16)
    grad_w_second = jnp.einsum(
        "njsw,njsv->jwv", act_first, delta_second, preferred_element_type=jnp.float32
    )
    grad_b_second = jnp.sum(delta_second, axis=(0, 2), dtype=jnp.float32)
    back_first = jnp.einsum(
        "njsv,jwv->njsw", delta_second, w_second, preferred_element_type=jnp.float32
    )
    delta_first = (back_first * silu_slope(pre_first)).astype(jnp.bfloat16)
    grad_w_first = jnp.einsum(
        "njse,njsw->jew", encoded, delta_first, preferred_element_type=jnp.float32
    )
    grad_b_first = jnp.sum(delta_first, axis=(0, 2), dtype=jnp.float32)

    def code_sums(cell_index):
        table = code_table(code_ids, cell_index, codes_total)
        color_slopes = slopes[:, cell_index, :, 1:4].reshape(-1, 3)
        return jnp.einsum("mc,mk->ck", table, color_slopes, preferred_element_type=jnp.float32)

    per_code = lax.map(code_sums, jnp.arange(cell_dev, dtype=jnp.int32))
    grad_head_app = jnp.einsum("jck,ac->jka", per_code, app_table, precision=lax.Precision.HIGHEST)
    table_part = jnp.einsum(
        "jka,jck->ac", head_app.astype(jnp.float32), per_code, precision=lax.Precision.HIGHEST
    )
    grad_table = lax.psum(table_part, "cell")
    return (
        grad_w_first,
        grad_b_first,
        grad_w_second,
        grad_b_second,
        grad_head_out,
        grad_head_app,
        grad_table,
    )


def solution(mesh):
    placed = (
        P(None, ("groups", "cell")),
        P(("groups", "cell")),
        P(None, ("groups", "cell")),
        P(None, ("groups", "cell")),
        P(("groups", "cell")),
        P(),
        P("cell", None, None),
        P("cell", None),
        P("cell", None, None),
        P("cell", None),
        P("cell", None, None),
        P("cell", None, None),
        P(),
        P(("groups", "cell"), None),
        P(("groups", "cell")),
    )
    return jax.shard_map(
        local,
        mesh=mesh,
        in_specs=placed,
        out_specs=(
            P(("groups", "cell"), None, None),
            P(("groups", "cell"), None),
            P(("groups", "cell"), None, None),
            P(("groups", "cell"), None),
            P(("groups", "cell"), None, None),
            P(("groups", "cell"), None, None),
            P("groups", None),
        ),
        check_vma=False,
    )
```

profile of v0, /device:TPU:0, one launch (start us, length us, event | category | flops | bytes accessed | tf_op | source)
XLA Modules:
  0.0 445.7 jit_solution(7194965841063556286)
XLA Ops:
  7.2 2.1 fusion.77
  9.3 1.6 fusion.78
  10.8 2.1 fusion.75
  12.9 2.1 fusion.76
  15.8 4.6 %compare_select_fusion.5 = (s32[6144,1]{0,1:T(1,128)S(1)}, s32[6144,1]{0,1:T(1,128)S(1)}, s32[6144,1]{0,1:T(1,128)S(1)}) fusion(s32[]{:T(128)} %bitcast.77, s32[]{:T(128)} %bitcast.78, s32[]{:T(128)} %bitcast.79, s32[]{:T(128)} %bitcast.80, s32[]{:T(128)} %bitcast.81, s32[]{:T(128)} %bitcast.83, s32[]{:T(128)} %bitcast.82, s32[6144,1]{0,1:T(1,128)S(1)} %reshape.212), kind=kLoop, calls=%fused_computation.142 | loop fusion | flops 159744 | bytes 98332 | tf_op jit(solution)/shard_map/gather | solution.py:106
  20.4 4.4 compare_reduce_fusion.56
  24.8 36.0 %select_select_fusion = s32[6144]{0:T(1024)S(1)} fusion(pred[6144]{0:T(1024)(128)(4,1)S(1)} %get-tuple-element.187, pred[6144]{0:T(1024)(128)(4,1)S(1)} %get-tuple-element.186, pred[6144]{0:T(1024)(128)(4,1)S(1)} %get-tuple-element.185, pred[6144]{0:T(1024)(128)(4,1)S(1)} %get-tuple-element.184, pred[6144]{0:T(1024)(128)(4,1)S(1)} %get-tuple-element.183, ...), kind=kLoop, calls=%fused_computation.173 | loop fusion | flops 350208 | bytes 399588 | tf_op jit(solution)/shard_map/gather | solution.py:106
  61.5 7.6 %all-to-all-start.1 = ((s32[16,2,192]{2,1,0:T(2,128)}), s32[16,2,192]{2,1,0:T(2,128)}, u32[]{:S(2)}, u32[]{:S(2)}) async-start(s32[16,2,192]{2,1,0:T(2,128)} %reshape.214), calls=%async_computation.1 | async-start | bytes 65536 | tf_op jit(solution)/shard_map/all_to_all | solution.py:118
  70.0 3.0 copy.94
  73.6 20.9 %gather_fusion = f32[6144,3]{1,0:T(8,128)S(1)} fusion(f32[3,6144]{0,1:T(8,128)} %copy.94, s32[6144]{0:T(1024)} %broadcast_clamp_fusion), kind=kCustom, calls=%fused_computation | custom fusion | bytes 172032 | tf_op jit(solution)/shard_map/gather | solution.py:114
  94.5 4.7 %slice_reduce_fusion.2 = (f32[6144]{0:T(1024)}, f32[6144]{0:T(1024)}, f32[6144]{0:T(1024)}) fusion(f32[3,6144]{0,1:T(8,128)S(1)} %bitcast.277), kind=kLoop, calls=%fused_computation.47 | loop fusion | bytes 147456 | tf_op jit(solution)/shard_map/slice | solution.py:115
  101.7 12.3 %sine_convert_fusion = (bf16[16,2,192,64]{3,2,1,0:T(8,128)(2,1)S(1)}, bf16[16,2,192,64]{3,2,1,0:T(8,128)(2,1)S(1)}) fusion(f32[64]{0:T(128)S(1)} %get-tuple-element.220, f32[16,2,192]{2,1,0:T(2,128)S(1)} %mul.146, f32[64]{0:T(128)S(1)} %get-tuple-element.221, f32[16,2,192]{2,1,0:T(2,128)S(1)} %mul.141, f32[64]{0:T(128)S(1)} %get-tuple-element.219, ...), kind=kLoop, calls=%fused_computation.53 | loop fusion | flops 2752512 | bytes 1647360 | tf_op jit(solution)/shard_map/convert.3
  114.0 2.0 pad_maximum_fusion
  116.0 6.1 %all-to-all-start = ((bf16[16,2,192,128]{3,2,1,0:T(8,128)(2,1)}), bf16[16,2,192,128]{3,2,1,0:T(8,128)(2,1)S(1)}, u32[]{:S(2)}, u32[]{:S(2)}) async-start(bf16[16,2,192,128]{3,2,1,0:T(8,128)(2,1)} %pad_maximum_fusion), calls=%async_computation | async-start | bytes 3145728 | tf_op jit(solution)/shard_map/all_to_all | solution.py:117
  122.1 23.2 %scatter_custom_fusion = s32[6144]{0:T(1024)S(1)} fusion(s32[6144]{0:T(1024)} %bitcast.286, s32[6144]{0:T(1024)S(1)} %iota.21, s32[]{:T(128)} %constant.31.clone.1), kind=kCustom, calls=%fused_computation.175 | custom fusion | bytes 25088 | tf_op jit(solution)/shard_map/scatter | solution.py:104
  145.7 29.5 %while.20 = (s32[]{:T(128)}, f32[2,3072,3]{1,2,0:T(4,128)S(1)}, s32[2]{0:T(128)S(1)}, s32[16,2,192]{2,1,0:T(2,128)}, f32[2,2048,3]{1,2,0:T(4,128)S(1)}, /*index=5*/s32[]{:T(128)}, s32[]{:T(128)}, s32[]{:T(128)}) while((s32[]{:T(128)}, f32[2,3072,3]{1,2,0:T(4,128)S(1)}, s32[2]{0:T(128)S(1)}, s32[16,2,192]{2,1,0:T(2,128)}, ...), condition=%wide.region_2.3_spmd, body=%wide.region_1.2_spmd.sunk | while | flops 232783872 | bytes 143511 | solution.py:53
  149.3 11.2 %fusion.94 = f32[2,3072,3]{1,2,0:T(4,128)S(1)} fusion(f32[2,3072,3]{1,2,0:T(4,128)S(1)} %get-tuple-element.365, s32[]{:T(128)S(6)} %copy.181, s32[3072]{0:T(1024)S(1)} %eq.103, f32[2,2048,3]{1,2,0:T(4,128)S(1)} %get-tuple-element.376, s32[]{:T(128)S(6)} %select_n.97), kind=kOutput, calls=%fused_computation.9.clone.1 | convolution fusion | flops 232783872 | bytes 94216 | tf_op jit(solution)/shard_map/while/body/eval_jaxpr/dot_general | solution.py:46
  164.0 11.2 %fusion.94 = f32[2,3072,3]{1,2,0:T(4,128)S(1)} fusion(f32[2,3072,3]{1,2,0:T(4,128)S(1)} %get-tuple-element.365, s32[]{:T(128)S(6)} %copy.181, s32[3072]{0:T(1024)S(1)} %eq.103, f32[2,2048,3]{1,2,0:T(4,128)S(1)} %get-tuple-element.376, s32[]{:T(128)S(6)} %select_n.97), kind=kOutput, calls=%fused_computation.9.clone.1 | convolution fusion | flops 232783872 | bytes 94216 | tf_op jit(solution)/shard_map/while/body/eval_jaxpr/dot_general | solution.py:46
  175.5 3.6 fusion.22
  179.1 4.4 fusion.16
  183.5 1.7 copy-done.1
  186.8 6.3 %all-to-all-start.2 = ((bf16[16,2,192,4]{2,3,1,0:T(4,128)(2,1)}), bf16[16,2,192,4]{2,3,1,0:T(4,128)(2,1)S(1)}, u32[]{:S(2)}, u32[]{:S(2)}) async-start(bf16[16,2,192,4]{2,3,1,0:T(4,128)(2,1)} %copy.99), calls=%async_computation.2 | async-start | bytes 131072 | tf_op jit(solution)/shard_map/all_to_all | solution.py:125
  193.2 34.3 %gather_fusion.1 = f32[6144]{0:T(1024)S(1)} fusion(f32[6144]{0:T(1024)S(1)} %reshape.221, s32[6144]{0:T(1024)S(1)} %fusion.61), kind=kCustom, calls=%fused_computation.1 | custom fusion | bytes 73728 | tf_op jit(solution)/shard_map/gather | solution.py:110
  230.0 21.0 %gather_fusion.2 = bf16[6144,4]{1,0:T(8,128)(2,1)S(1)} fusion(bf16[4,6144]{0,1:T(8,128)(2,1)S(1)} %bitcast.280, s32[6144]{0:T(1024)} %copy-done.7), kind=kCustom, calls=%fused_computation.2 | custom fusion | bytes 122880 | tf_op jit(solution)/shard_map/gather | solution.py:126
  251.0 2.1 slice.116
  253.1 2.2 slice.118
  255.3 3.1 copy.170
  258.5 1.5 copy.145
  259.9 1.5 fusion.59
  261.5 1.5 copy.106
  263.0 1.6 reduce_window_sum.22
  264.6 1.4 slice.119
  266.0 1.5 copy.146
  267.5 1.5 fusion.73
  271.5 1.8 copy.171
  281.7 21.0 %gather_fusion.3 = bf16[6144,4]{1,0:T(8,128)(2,1)S(1)} fusion(bf16[4,6144]{0,1:T(8,128)(2,1)S(1)} %bitcast.281, s32[6144]{0:T(1024)} %broadcast_clamp_fusion), kind=kCustom, calls=%fused_computation.3 | custom fusion | bytes 122880 | tf_op jit(solution)/shard_map/gather | solution.py:135
  302.8 1.5 copy.117
  304.3 6.0 %all-to-all-start.3 = ((bf16[16,2,192,4]{2,3,1,0:T(4,128)(2,1)}), bf16[16,2,192,4]{2,3,1,0:T(4,128)(2,1)S(1)}, u32[]{:S(2)}, u32[]{:S(2)}) async-start(bf16[16,2,192,4]{2,3,1,0:T(4,128)(2,1)} %copy.117), calls=%async_computation.3 | async-start | bytes 131072 | tf_op jit(solution)/shard_map/all_to_all | solution.py:137
  310.4 6.8 %all-to-all-done.3 = bf16[16,2,192,4]{2,3,1,0:T(4,128)(2,1)S(1)} async-done(((bf16[16,2,192,4]{2,3,1,0:T(4,128)(2,1)}), bf16[16,2,192,4]{2,3,1,0:T(4,128)(2,1)S(1)}, u32[]{:S(2)}, u32[]{:S(2)}) %all-to-all-start.3) | async-done | bytes 49184 | tf_op jit(solution)/shard_map/all_to_all | solution.py:137
  317.2 15.3 %while.21 = (s32[]{:T(128)}, f32[2,2048,3]{1,2,0:T(4,128)S(1)}, s32[2]{0:T(128)S(1)}, s32[16,2,192]{2,1,0:T(2,128)}, bf16[16,2,192,4]{2,0,3,1:T(8,128)(2,1)S(1)}, /*index=5*/s32[]{:T(128)}, s32[]{:T(128)}, s32[]{:T(128)}) while((s32[]{:T(128)}, f32[2,2048,3]{1,2,0:T(4,128)S(1)}, s32[2]{0:T(128)S(1)}, s32[16,2,192]{2,1,0:T(2,128)}, ...), condition=%wide.region_9.10_spmd, body=%wide.region_8.9_spmd.sunk | while | flops 44040196 | bytes 192663 | solution.py:167
  320.8 4.1 fusion.96
  328.4 4.1 fusion.96
  334.2 5.5 %convert_reduce_fusion = (f32[2,256]{1,0:T(2,128)}, bf16[16,2,192,256]{3,2,0,1:T(8,128)(2,1)S(1)}) fusion(f32[2,16,192,256]{3,2,1,0:T(8,128)} %get-tuple-element.289, f32[2,256]{1,0:T(2,128)S(1)} %copy-done.19, bf16[2,4,256]{2,1,0:T(4,128)(2,1)S(1)} %copy-done.11, bf16[16,2,192,4]{2,3,1,0:T(4,128)(2,1)S(1)} %all-to-all-done.3), kind=kOutput, calls=%fused_computation.43 | convolution fusion | flops 31456768 | bytes 9494528 | tf_op jit(solution)/shard_map/njso,jow->njsw/dot_general | solution.py:147
  339.6 2.2 convolution_bitcast_fusion.2
  341.8 6.5 %convert_reduce_fusion.1 = (f32[2,256]{1,0:T(2,128)}, bf16[16,2,192,256]{3,2,0,1:T(8,128)(2,1)}) fusion(f32[2,16,192,256]{3,2,1,0:T(8,128)} %get-tuple-element.287, f32[2,256]{1,0:T(2,128)S(1)} %copy-done.21, bf16[16,2,192,256]{3,2,0,1:T(8,128)(2,1)S(1)} %get-tuple-element.293, bf16[2,256,256]{2,1,0:T(8,128)(2,1)S(1)} %copy-done.16), kind=kOutput, calls=%fused_computation.44 | convolution fusion | flops 824180224 | bytes 12849152 | tf_op jit(solution)/shard_map/njsv,jwv->njsw/dot_general | solution.py:153
  348.9 4.1 fusion.31
  354.2 82.5 %all-reduce.8.cloned.1.call-done = f32[48,2048]{1,0:T(8,128)} async-done(((f32[48,2048]{1,0:T(8,128)}), f32[48,2048]{1,0:T(8,128)}) %all-reduce.8.cloned.1.call-update) | async-done | bytes 393232 | tf_op jit(solution)/shard_map/psum | solution.py:172
  436.7 1.8 copy.192
  (114 shorter events, 30.6 us)
Async XLA Ops:
  7.2 138.2 %copy-start = (f32[48,2048]{1,0:T(8,128)S(1)}, f32[48,2048]{1,0:T(8,128)}, u32[]{:S(2)}) copy-start(f32[48,2048]{1,0:T(8,128)} %param.31) | copy-start | bytes 1179652
  20.4 52.5 %copy-start.8 = (s32[6144,1]{0,1:T(1,128)}, s32[6144,1]{0,1:T(1,128)S(1)}, u32[]{:S(2)}) copy-start(s32[6144,1]{0,1:T(1,128)S(1)} %get-tuple-element.216) | copy-start | bytes 73732
  61.5 54.5 %all-to-all-start.1 = ((s32[16,2,192]{2,1,0:T(2,128)}), s32[16,2,192]{2,1,0:T(2,128)}, u32[]{:S(2)}, u32[]{:S(2)}) async-start(s32[16,2,192]{2,1,0:T(2,128)} %reshape.214), calls=%async_computation.1 | async-start | bytes 65536 | tf_op jit(solution)/shard_map/all_to_all | solution.py:118
  114.0 31.4 %copy-start.10 = (bf16[2,3,48]{2,0,1:T(2,128)(2,1)S(1)}, bf16[2,3,48]{2,0,1:T(2,128)(2,1)}, u32[]{:S(2)}) copy-start(bf16[2,3,48]{2,0,1:T(2,128)(2,1)} %param.30) | copy-start | bytes 1732
  116.0 59.4 %all-to-all-start = ((bf16[16,2,192,128]{3,2,1,0:T(8,128)(2,1)}), bf16[16,2,192,128]{3,2,1,0:T(8,128)(2,1)S(1)}, u32[]{:S(2)}, u32[]{:S(2)}) async-start(bf16[16,2,192,128]{3,2,1,0:T(8,128)(2,1)} %pad_maximum_fusion), calls=%async_computation | async-start | bytes 3145728 | tf_op jit(solution)/shard_map/all_to_all | solution.py:117
  145.4 47.8 %copy-start.7 = (s32[6144]{0:T(1024)}, s32[6144]{0:T(1024)S(1)}, u32[]{:S(2)}) copy-start(s32[6144]{0:T(1024)S(1)} %fusion.61) | copy-start | bytes 73732
  145.6 29.8 %copy-start.17 = (bf16[2,128,256]{2,1,0:T(8,128)(2,1)S(1)}, bf16[2,128,256]{2,1,0:T(8,128)(2,1)}, u32[]{:S(2)}) copy-start(bf16[2,128,256]{2,1,0:T(8,128)(2,1)} %param.25) | copy-start | bytes 393220
  145.7 29.8 %copy-start.20 = (f32[2,256]{1,0:T(2,128)S(1)}, f32[2,256]{1,0:T(2,128)}, u32[]{:S(2)}) copy-start(f32[2,256]{1,0:T(2,128)} %param.26) | copy-start | bytes 6148
  175.4 3.7 copy-start.15
  175.4 3.7 copy-start.18
  175.4 3.6 copy-start.4
  179.1 4.5 copy-start.22
  179.1 6.1 %copy-start.11 = (bf16[2,4,256]{2,1,0:T(4,128)(2,1)S(1)}, bf16[2,4,256]{2,1,0:T(4,128)(2,1)}, u32[]{:S(2)}) copy-start(bf16[2,4,256]{2,1,0:T(4,128)(2,1)} %param.29) | copy-start | bytes 12292
  183.5 1.7 copy-start.1
  183.5 9.5 %copy-start.14 = (s32[32]{0:T(128)S(1)}, s32[32]{0:T(128)}, u32[]{:S(2)}) copy-start(s32[32]{0:T(128)} %param.33) | copy-start | bytes 388
  186.8 42.3 %all-to-all-start.2 = ((bf16[16,2,192,4]{2,3,1,0:T(4,128)(2,1)}), bf16[16,2,192,4]{2,3,1,0:T(4,128)(2,1)S(1)}, u32[]{:S(2)}, u32[]{:S(2)}) async-start(bf16[16,2,192,4]{2,3,1,0:T(4,128)(2,1)} %copy.99), calls=%async_computation.2 | async-start | bytes 131072 | tf_op jit(solution)/shard_map/all_to_all | solution.py:125
  193.2 35.1 %copy-start.9 = (f32[6144]{0:T(1024)S(1)}, f32[6144]{0:T(1024)}, u32[]{:S(2)}) copy-start(f32[6144]{0:T(1024)} %param.20) | copy-start | bytes 73732
  255.3 16.2 %copy-start.3 = (f32[64,96,3]{2,1,0:T(8,128)S(1)}, f32[64,96,3]{2,1,0:T(8,128)}, u32[]{:S(2)}) copy-start(f32[64,96,3]{2,1,0:T(8,128)} %slice.118) | copy-start | bytes 221188
  255.3 19.9 %copy-start.12 = (f32[3,64]{1,0:T(4,128)S(1)}, f32[3,64]{1,0:T(4,128)}, u32[]{:S(2)}) copy-start(f32[3,64]{1,0:T(4,128)} %param.21) | copy-start | bytes 2308
  255.3 19.9 %copy-start.13 = (f32[3,64]{1,0:T(4,128)S(1)}, f32[3,64]{1,0:T(4,128)}, u32[]{:S(2)}) copy-start(f32[3,64]{1,0:T(4,128)} %param.22) | copy-start | bytes 2308
  304.3 12.9 %all-to-all-start.3 = ((bf16[16,2,192,4]{2,3,1,0:T(4,128)(2,1)}), bf16[16,2,192,4]{2,3,1,0:T(4,128)(2,1)S(1)}, u32[]{:S(2)}, u32[]{:S(2)}) async-start(bf16[16,2,192,4]{2,3,1,0:T(4,128)(2,1)} %copy.117), calls=%async_computation.3 | async-start | bytes 131072 | tf_op jit(solution)/shard_map/all_to_all | solution.py:137
  310.3 126.4 %all-reduce.8.cloned.1.call-start = ((), (), s32[]{:S(2)}) async-start(), calls=%async_computation.4 | async-start | bytes 786432 | tf_op jit(solution)/shard_map/psum | solution.py:172
  317.2 17.0 %copy-start.5 = (bf16[16,2,192,4]{2,3,1,0:T(4,128)(2,1)}, bf16[16,2,192,4]{2,3,1,0:T(4,128)(2,1)S(1)}, u32[]{:S(2)}) copy-start(bf16[16,2,192,4]{2,3,1,0:T(4,128)(2,1)S(1)} %all-to-all-done.3) | copy-start | bytes 147460
  317.2 16.9 %copy-start.19 = (f32[2,256]{1,0:T(2,128)S(1)}, f32[2,256]{1,0:T(2,128)}, u32[]{:S(2)}) copy-start(f32[2,256]{1,0:T(2,128)} %param.28) | copy-start | bytes 6148
  334.2 5.5 %copy-start.23 = (bf16[16,2,192,256]{3,2,0,1:T(8,128)(2,1)S(1)}, bf16[16,2,192,256]{3,2,0,1:T(8,128)(2,1)}, u32[]{:S(2)}) copy-start(bf16[16,2,192,256]{3,2,0,1:T(8,128)(2,1)} %copy-done.22) | copy-start | bytes 9437188
  339.6 2.2 copy-start.16
  339.6 2.2 copy-start.21
  348.3 4.8 %copy-start.2 = (bf16[16,2,192,256]{3,2,0,1:T(8,128)(2,1)S(1)}, bf16[16,2,192,256]{3,2,0,1:T(8,128)(2,1)}, u32[]{:S(2)}) copy-start(bf16[16,2,192,256]{3,2,0,1:T(8,128)(2,1)} %copy-done.1) | copy-start | bytes 9437188
  348.9 4.2 copy-start.6
Sparse Core Ops, SparseCore 0:
  349.0 87.6 all-reduce.7
where the time goes:
time: 454 us; the launch traced here: 446 us
  local copies, waits for them, and re-layouts  175 us (39%)
  waiting for transfers between devices  89.3 us (20%)
  other arithmetic  71.6 us (16%)
  matrix products  60.9 us (13%)
  starting transfers between devices  26 us (6%)
  between operations  14.9 us (3%)
  loops' own time  8.05 us (2%)
    psum x1, waiting for transfers between devices, local(): grad_table = lax.psum(table_part, 'cell')  82.5 us
    gather x3, other arithmetic, local(): ray_codes[listed // samples].reshape(cell_axis_size, cell_dev, capacity)  45 us
    gather x1, local copies, waits for them, and re-layouts, local(): routed = live_mask.reshape(-1)[inverse]  34.3 us
    scatter x1, local copies, waits for them, and re-layouts, local(): jnp.zeros((rows_local,), jnp.int32).at[listed]  23.2 us
    dot_general x2, matrix products, one_cell(): jnp.dot(table, projected[cell_index], precision=lax.Precision.HIGHEST, pr...  22.4 us
    gather x1, local copies, waits for them, and re-layouts, local(): raw_columns = raw_back.reshape(-1, 4).T[:, inverse]  21 us
    gather x1, local copies, waits for them, and re-layouts, local(): slope_rows.reshape(rows_local, 4).astype(jnp.bfloat16).T[:, listed]  21 us
    gather x1, local copies, waits for them, and re-layouts, local(): slot_positions = positions[:, listed]  20.9 us
  transfers between devices with their start and end apart: 5, of which 2 were waited for; matrix products, arithmetic and copies ran while one was open for 31% of the time, Pallas kernels for 0%

commit v1 on v0

v1 whole, which is shorter than its diff:
```python
import jax
import jax.numpy as jnp
from jax import lax
from jax.experimental import pallas as pl
from jax.experimental.pallas import tpu as pltpu
from jax.sharding import PartitionSpec as P

loss_scale = 256.0
F32 = jnp.float32
BF16 = jnp.bfloat16
HIGH = lax.Precision.HIGHEST
PARAMS = pltpu.CompilerParams(vmem_limit_bytes=48 * 1024 * 1024)


def nn(a, b, precision=None):
    return lax.dot_general(
        a, b, (((1,), (0,)), ((), ())), precision=precision, preferred_element_type=F32
    )


def nt(a, b, precision=None):
    return lax.dot_general(
        a, b, (((1,), (1,)), ((), ())), precision=precision, preferred_element_type=F32
    )


def tn(a, b, precision=None):
    return lax.dot_general(
        a, b, (((0,), (0,)), ((), ())), precision=precision, preferred_element_type=F32
    )


def chunk_of(total, most):
    best = total
    for size in range(128, most + 1, 128):
        if total % size == 0:
            best = size
    return best


def split3(value):
    high = value.astype(BF16)
    rest = value - high.astype(F32)
    mid = rest.astype(BF16)
    low = (rest - mid.astype(F32)).astype(BF16)
    return high, mid, low


def one_hot(index_row, depth):
    rows = lax.broadcasted_iota(jnp.int32, (depth, index_row.shape[1]), 0)
    return rows == index_row


def hot_bf16(mask):
    return jnp.where(mask, 1.0, 0.0).astype(BF16)


def sigmoid(value):
    return 0.5 * jnp.tanh(0.5 * value) + 0.5


PI_A = 3.140625
PI_B = 9.676535897932e-4


def sine(angle, shift):
    turns = jnp.round(angle * 0.3183098861837907 + shift)
    whole = turns - shift
    rest = (angle - whole * PI_A) - whole * PI_B
    odd = turns - 2.0 * jnp.floor(turns * 0.5)
    rest = rest * (1.0 - 2.0 * odd)
    square = rest * rest
    poly = -2.5052108e-8
    poly = poly * square + 2.7557319e-6
    poly = poly * square - 1.9841270e-4
    poly = poly * square + 8.3333333e-3
    poly = poly * square - 1.6666667e-1
    return rest + rest * square * poly


def pick_kernel(ray_ref, sam_ref, pos_ref, codes_ref, table_ref, slot_ref, app_ref):
    samples = pos_ref.shape[1]
    rays = pos_ref.shape[2]
    slots = ray_ref.shape[1]
    chunk = chunk_of(slots, 1024)
    codes_total = table_ref.shape[1]
    stacked = pos_ref[...].reshape(3 * samples, rays)
    parts = split3(stacked)
    code_hot = jnp.where(one_hot(codes_ref[...], codes_total), 1.0, 0.0).astype(BF16)
    table_parts = split3(table_ref[...])
    app_ref[...] = (nn(table_parts[2], code_hot) + nn(table_parts[1], code_hot)) + nn(
        table_parts[0], code_hot
    )

    def body(step, carry):
        here = pl.ds(pl.multiple_of(step * chunk, 128), chunk)
        ray_hot = hot_bf16(one_hot(ray_ref[:, here], rays))
        sam_hot = one_hot(sam_ref[:, here], samples)
        picked = (nn(parts[2], ray_hot) + nn(parts[1], ray_hot)) + nn(parts[0], ray_hot)
        for axis in range(3):
            part = picked[axis * samples : (axis + 1) * samples]
            slot_ref[axis : axis + 1, here] = jnp.sum(
                jnp.where(sam_hot, part, 0.0), axis=0, keepdims=True
            )
        return carry

    lax.fori_loop(0, slots // chunk, body, 0)


def encode_block(pos, freq):
    angle = pos[0:1] * freq[:, 0:1] + pos[1:2] * freq[:, 1:2]
    angle = angle + pos[2:3] * freq[:, 2:3]
    return jnp.concatenate([sine(angle, 0.0), sine(angle, 0.5)], axis=0).astype(BF16)


def network(pos_ref, freq_ref, w1_ref, b1_ref, w2_ref, b2_ref):
    encoded = encode_block(pos_ref[0], freq_ref[...])
    pre_first = tn(w1_ref[0], encoded) + b1_ref[0]
    sig_first = sigmoid(pre_first)
    act_first = (pre_first * sig_first).astype(BF16)
    pre_second = tn(w2_ref[0], act_first) + b2_ref[0]
    sig_second = sigmoid(pre_second)
    act_second = (pre_second * sig_second).astype(BF16)
    return encoded, pre_first, sig_first, act_first, pre_second, sig_second, act_second


def forward_kernel(pos_ref, freq_ref, w1_ref, b1_ref, w2_ref, b2_ref, head_ref, out_ref):
    act_second = network(pos_ref, freq_ref, w1_ref, b1_ref, w2_ref, b2_ref)[6]
    out_ref[0] = nn(head_ref[0], act_second)


def backward_kernel(
    pos_ref,
    freq_ref,
    w1_ref,
    b1_ref,
    w2_ref,
    b2_ref,
    head_ref,
    slope_ref,
    gw1_ref,
    gb1_ref,
    gw2_ref,
    gb2_ref,
    gh_ref,
):
    encoded, pre_first, sig_first, act_first, pre_second, sig_second, act_second = network(
        pos_ref, freq_ref, w1_ref, b1_ref, w2_ref, b2_ref
    )
    slopes = slope_ref[0].astype(BF16)

    @pl.when(pl.program_id(1) == 0)
    def _():
        for ref in (gw1_ref, gb1_ref, gw2_ref, gb2_ref, gh_ref):
            ref[...] = jnp.zeros_like(ref)

    ones = jnp.ones((8, slopes.shape[1]), BF16)
    gh_ref[0] += nt(slopes, act_second)
    back_second = tn(head_ref[0], slopes)
    delta_second = (
        back_second * (sig_second * (1.0 + pre_second * (1.0 - sig_second)))
    ).astype(BF16)
    gw2_ref[0] += nt(act_first, delta_second)
    gb2_ref[0] += nt(ones, delta_second)[0:1]
    back_first = nn(w2_ref[0], delta_second)
    delta_first = (back_first * (sig_first * (1.0 + pre_first * (1.0 - sig_first)))).astype(BF16)
    gw1_ref[0] += nt(encoded, delta_first)
    gb1_ref[0] += nt(ones, delta_first)[0:1]


def ray_kernel(
    ray_ref,
    sam_ref,
    cell_ref,
    live_ref,
    outs_ref,
    heads_ref,
    app_ref,
    deltas_ref,
    back_ref,
    target_ref,
    slope_ref,
    partial_ref,
    code_ref,
    shift_ref,
    rows_ref,
    sums_ref,
):
    samples, rays = deltas_ref.shape
    slots = ray_ref.shape[1]
    cells = heads_ref.shape[0] // 3
    chunk = chunk_of(slots, 512)
    steps = slots // chunk
    shift_ref[...] = nn(heads_ref[...], app_ref[...], HIGH)
    rows_ref[...] = jnp.zeros_like(rows_ref)
    shift_parts = split3(shift_ref[...])

    def gather_rows(step, carry):
        here = pl.ds(pl.multiple_of(step * chunk, 128), chunk)
        ray_hot = hot_bf16(one_hot(ray_ref[:, here], rays))
        sam_hot = one_hot(sam_ref[:, here], samples)
        cell_hot = one_hot(cell_ref[:, here], cells)
        shifts = (nn(shift_parts[2], ray_hot) + nn(shift_parts[1], ray_hot)) + nn(
            shift_parts[0], ray_hot
        )
        columns = [outs_ref[0:1, here]]
        for k in range(3):
            part = shifts[k * cells : (k + 1) * cells]
            picked = jnp.sum(jnp.where(cell_hot, part, 0.0), axis=0, keepdims=True)
            columns.append(outs_ref[k + 1 : k + 2, here] + picked)
        columns.append(live_ref[:, here])
        spread = [jnp.where(sam_hot, column, 0.0).astype(BF16) for column in columns]
        rows_ref[...] += nt(jnp.concatenate(spread, axis=0), ray_hot)
        return carry

    lax.fori_loop(0, steps, gather_rows, 0)
    raw = [rows_ref[k * samples : (k + 1) * samples] for k in range(4)]
    routed = rows_ref[4 * samples : 5 * samples]
    deltas = deltas_ref[...]
    first = lax.broadcasted_iota(jnp.int32, (samples, samples), 0)
    second = lax.broadcasted_iota(jnp.int32, (samples, samples), 1)
    earlier = jnp.where(second < first, 1.0, 0.0)
    later = jnp.where(second > first, 1.0, 0.0)
    tail = jnp.exp(-jnp.abs(raw[0]))
    softplus = jnp.maximum(raw[0], 0.0) + jnp.log1p(tail)
    optical = routed * softplus * deltas
    before = nn(earlier, optical, HIGH)
    total = jnp.sum(optical, axis=0, keepdims=True)
    through = jnp.exp(-before)
    kept = jnp.exp(-optical)
    weight = through * (1.0 - kept)
    leaving = jnp.exp(-total)
    back_slope = jnp.zeros_like(total)
    weight_slope = jnp.zeros_like(weight)
    slope_parts = []
    for k in range(3):
        color = jax.nn.sigmoid(raw[k + 1])
        pixel = jnp.sum(weight * color, axis=0, keepdims=True) + leaving * back_ref[k : k + 1]
        pixel_slope = loss_scale * (pixel - target_ref[k : k + 1])
        back_slope = back_slope + pixel_slope * back_ref[k : k + 1]
        weight_slope = weight_slope + pixel_slope * color
        slope_parts.append((weight * pixel_slope * (color * (1.0 - color))).astype(BF16))
    after = nn(later, weight_slope * weight, HIGH)
    optical_slope = weight_slope * through * kept - after - leaving * back_slope
    density_slope = optical_slope * deltas * routed * jax.nn.sigmoid(raw[0])
    stacked = jnp.concatenate([density_slope.astype(BF16)] + slope_parts, axis=0)
    sums_ref[...] = jnp.zeros_like(sums_ref)

    def spread_slopes(step, carry):
        here = pl.ds(pl.multiple_of(step * chunk, 128), chunk)
        ray_hot = hot_bf16(one_hot(ray_ref[:, here], rays))
        sam_hot = one_hot(sam_ref[:, here], samples)
        cell_hot = one_hot(cell_ref[:, here], cells)
        picked = nn(stacked, ray_hot)
        spread = []
        for k in range(4):
            part = picked[k * samples : (k + 1) * samples]
            column = jnp.sum(jnp.where(sam_hot, part, 0.0), axis=0, keepdims=True)
            slope_ref[k : k + 1, here] = column
            if k:
                spread.append(jnp.where(cell_hot, column, 0.0).astype(BF16))
        sums_ref[...] += nt(jnp.concatenate(spread, axis=0), ray_hot)
        return carry

    lax.fori_loop(0, steps, spread_slopes, 0)
    sums = sums_ref[...]
    partial_ref[...] = nt(sums, app_ref[...], HIGH)
    code_ref[...] = tn(heads_ref[...], sums, HIGH)


def table_kernel(codes_ref, terms_ref, out_ref):
    codes_block = out_ref.shape[1]
    base = pl.program_id(0) * codes_block
    rows = lax.broadcasted_iota(jnp.int32, (codes_block, codes_ref.shape[1]), 0) + base
    hot = hot_bf16(rows == codes_ref[...])
    parts = split3(terms_ref[...])
    out_ref[...] = (nt(parts[2], hot) + nt(parts[1], hot)) + nt(parts[0], hot)


def local(
    positions,
    deltas,
    background,
    target,
    ray_codes,
    frequencies,
    w_first,
    b_first,
    w_second,
    b_second,
    head_out,
    head_app,
    app_table,
    dispatch,
    counts,
):
    owners = lax.axis_size("cell")
    lists, capacity = dispatch.shape
    cell_dev, encoding, width = w_first.shape
    rows_local = positions.shape[1]
    rays = ray_codes.shape[0]
    samples = rows_local // rays
    app_width, codes_total = app_table.shape
    slots_cell = owners * capacity

    listed = dispatch.reshape(1, rows_local)
    slot_ray = listed // samples
    slot_sam = listed - slot_ray * samples
    slot_cell = lax.broadcasted_iota(jnp.int32, (lists, capacity), 0).reshape(1, rows_local)
    live = (jnp.arange(capacity, dtype=jnp.int32)[None, :] < counts[:, None]).astype(F32)
    live = live.reshape(1, rows_local)
    pos_grid = jnp.transpose(positions.reshape(3, rays, samples), (0, 2, 1))
    delta_grid = deltas.reshape(rays, samples).T

    slot_pos, app_rows = pl.pallas_call(
        pick_kernel,
        out_shape=(
            jax.ShapeDtypeStruct((3, rows_local), F32),
            jax.ShapeDtypeStruct((app_width, rays), F32),
        ),
        compiler_params=PARAMS,
        name="pick",
    )(slot_ray, slot_sam, pos_grid, ray_codes.reshape(1, rays), app_table)

    per_owner = cell_dev * capacity
    send = jnp.transpose(slot_pos.reshape(3, owners, per_owner), (1, 0, 2))
    extra = jnp.concatenate([head_app.astype(F32).reshape(-1), ray_codes.astype(F32)])
    extra = jnp.broadcast_to(extra[None, :], (owners, extra.shape[0]))
    message = jnp.concatenate([send.reshape(owners, 3 * per_owner), extra], axis=1)
    message = lax.all_to_all(message, "cell", split_axis=0, concat_axis=0, tiled=True)
    cell_pos = message[:, : 3 * per_owner].reshape(owners, 3, cell_dev, capacity)
    cell_pos = jnp.transpose(cell_pos, (2, 1, 0, 3)).reshape(cell_dev, 3, slots_cell)
    head_size = cell_dev * 3 * app_width
    heads = message[:, 3 * per_owner : 3 * per_owner + head_size]
    heads = jnp.transpose(heads.reshape(lists, 3, app_width), (1, 0, 2)).reshape(-1, app_width)
    all_codes = message[:, 3 * per_owner + head_size :].astype(jnp.int32).reshape(1, owners * rays)

    chunk = chunk_of(slots_cell, 1024)
    grid = (cell_dev, slots_cell // chunk)
    half = frequencies.shape[1]
    freq_columns = frequencies.T
    net_specs = [
        pl.BlockSpec((1, 3, chunk), lambda j, i: (j, 0, i)),
        pl.BlockSpec((half, 3), lambda j, i: (0, 0)),
        pl.BlockSpec((1, encoding, width), lambda j, i: (j, 0, 0)),
        pl.BlockSpec((1, width, 1), lambda j, i: (j, 0, 0)),
        pl.BlockSpec((1, width, width), lambda j, i: (j, 0, 0)),
        pl.BlockSpec((1, width, 1), lambda j, i: (j, 0, 0)),
        pl.BlockSpec((1, 4, width), lambda j, i: (j, 0, 0)),
    ]
    net_args = (
        cell_pos,
        freq_columns,
        w_first,
        b_first[:, :, None],
        w_second,
        b_second[:, :, None],
        head_out,
    )
    outputs = pl.pallas_call(
        forward_kernel,
        grid=grid,
        in_specs=net_specs,
        out_specs=pl.BlockSpec((1, 4, chunk), lambda j, i: (j, 0, i)),
        out_shape=jax.ShapeDtypeStruct((cell_dev, 4, slots_cell), F32),
        compiler_params=PARAMS,
        name="forward",
    )(*net_args)
    outputs = jnp.transpose(outputs.reshape(cell_dev, 4, owners, capacity), (2, 1, 0, 3))
    outputs = outputs.reshape(owners, 4 * per_owner)
    outputs = lax.all_to_all(outputs, "cell", split_axis=0, concat_axis=0, tiled=True)
    slot_outs = jnp.transpose(outputs.reshape(owners, 4, per_owner), (1, 0, 2))
    slot_outs = slot_outs.reshape(4, rows_local)

    slopes, partial, code_terms = pl.pallas_call(
        ray_kernel,
        out_shape=(
            jax.ShapeDtypeStruct((4, rows_local), F32),
            jax.ShapeDtypeStruct((3 * lists, app_width), F32),
            jax.ShapeDtypeStruct((app_width, rays), F32),
        ),
        scratch_shapes=[
            pltpu.VMEM((3 * lists, rays), F32),
            pltpu.VMEM((5 * samples, rays), F32),
            pltpu.VMEM((3 * lists, rays), F32),
        ],
        compiler_params=PARAMS,
        name="rays",
    )(
        slot_ray,
        slot_sam,
        slot_cell,
        live,
        slot_outs,
        heads,
        app_rows,
        delta_grid,
        background,
        target,
    )

    send = jnp.transpose(slopes.reshape(4, owners, per_owner), (1, 0, 2))
    partial = jnp.transpose(partial.reshape(3, lists, app_width), (1, 0, 2))
    message = jnp.concatenate(
        [
            send.reshape(owners, 4 * per_owner),
            partial.reshape(owners, head_size),
            jnp.broadcast_to(code_terms.reshape(1, -1), (owners, app_width * rays)),
        ],
        axis=1,
    )
    message = lax.all_to_all(message, "cell", split_axis=0, concat_axis=0, tiled=True)
    cell_slopes = message[:, : 4 * per_owner].reshape(owners, 4, cell_dev, capacity)
    cell_slopes = jnp.transpose(cell_slopes, (2, 1, 0, 3)).reshape(cell_dev, 4, slots_cell)
    grad_head_app = jnp.sum(message[:, 4 * per_owner : 4 * per_owner + head_size], axis=0)
    grad_head_app = grad_head_app.reshape(cell_dev, 3, app_width)
    terms = message[:, 4 * per_owner + head_size :].reshape(owners, app_width, rays)
    terms = jnp.transpose(terms, (1, 0, 2)).reshape(app_width, owners * rays)

    whole = lambda *dims: pl.BlockSpec((1,) + dims, lambda j, i: (j, 0, 0))
    grad_w_first, grad_b_first, grad_w_second, grad_b_second, grad_head_out = pl.pallas_call(
        backward_kernel,
        grid=grid,
        in_specs=net_specs + [pl.BlockSpec((1, 4, chunk), lambda j, i: (j, 0, i))],
        out_specs=(
            whole(encoding, width),
            whole(1, width),
            whole(width, width),
            whole(1, width),
            whole(4, width),
        ),
        out_shape=(
            jax.ShapeDtypeStruct((cell_dev, encoding, width), F32),
            jax.ShapeDtypeStruct((cell_dev, 1, width), F32),
            jax.ShapeDtypeStruct((cell_dev, width, width), F32),
            jax.ShapeDtypeStruct((cell_dev, 1, width), F32),
            jax.ShapeDtypeStruct((cell_dev, 4, width), F32),
        ),
        compiler_params=PARAMS,
        name="backward",
    )(*net_args, cell_slopes)

    block = chunk_of(codes_total, 512)
    grad_table = pl.pallas_call(
        table_kernel,
        grid=(codes_total // block,),
        in_specs=[
            pl.BlockSpec((1, owners * rays), lambda i: (0, 0)),
            pl.BlockSpec((app_width, owners * rays), lambda i: (0, 0)),
        ],
        out_specs=pl.BlockSpec((app_width, block), lambda i: (0, i)),
        out_shape=jax.ShapeDtypeStruct((app_width, codes_total), F32),
        compiler_params=PARAMS,
        name="table",
    )(all_codes, terms)
    return (
        grad_w_first,
        grad_b_first.reshape(cell_dev, width),
        grad_w_second,
        grad_b_second.reshape(cell_dev, width),
        grad_head_out,
        grad_head_app,
        grad_table,
    )


def solution(mesh):
    placed = (
        P(None, ("groups", "cell")),
        P(("groups", "cell")),
        P(None, ("groups", "cell")),
        P(None, ("groups", "cell")),
        P(("groups", "cell")),
        P(),
        P("cell", None, None),
        P("cell", None),
        P("cell", None, None),
        P("cell", None),
        P("cell", None, None),
        P("cell", None, None),
        P(),
        P(("groups", "cell"), None),
        P(("groups", "cell")),
    )
    return jax.shard_map(
        local,
        mesh=mesh,
        in_specs=placed,
        out_specs=(
            P(("groups", "cell"), None, None),
            P(("groups", "cell"), None),
            P(("groups", "cell"), None, None),
            P(("groups", "cell"), None),
            P(("groups", "cell"), None, None),
            P(("groups", "cell"), None, None),
            P("groups", None),
        ),
        check_vma=False,
    )
```

time: 454 us -> 94.1 us (0.21); the launches traced: 446 us -> 93.5 us
  local copies, waits for them, and re-layouts: 175 us -> 11.5 us
  other arithmetic: 71.6 us -> 1.35 us
  waiting for transfers between devices: 89.3 us -> 22.9 us
  matrix products: 60.9 us -> 0 us
  Pallas kernels: 0 us -> 42.1 us
  between operations: 14.9 us -> 1.01 us
  starting transfers between devices: 26 us -> 14.7 us
  loops' own time: 8.05 us -> 0 us
    gather x8 -> x0, local copies, waits for them, and re-layouts: 105 us -> none  [the longest x1 34.3 us: local(): routed = live_mask.reshape(-1)[inverse]]
    psum x1 -> x0, waiting for transfers between devices: 82.5 us -> none  [local(): grad_table = lax.psum(table_part, 'cell')]
    dot_general x15 -> x0, matrix products: 60.9 us -> none  [the longest x2 22.4 us: one_cell(): jnp.dot(table, projected[cell_index], precision=lax.Precision.HIGHEST, pr...]
    gather x5 -> x0, other arithmetic: 45.6 us -> none  [the longest x3 45 us: local(): ray_codes[listed // samples].reshape(cell_axis_size, cell_dev, capacity)]
    pallas_call x0 -> x5, Pallas kernels: none -> 42.1 us  [the longest x1 14.5 us: local(): pl.pallas_call(backward_kernel, grid=grid, in_specs=net_specs + [pl.Block...]
    scatter x1 -> x0, local copies, waits for them, and re-layouts: 23.2 us -> none  [local(): jnp.zeros((rows_local,), jnp.int32).at[listed]]
    all_to_all x4 -> x3, waiting for transfers between devices: 6.85 us -> 22.9 us  [the longest x2 15.9 us: local(): lax.all_to_all(message, 'cell', split_axis=0, concat_axis=0, tiled=True)]
    another operation x3 -> x0, other arithmetic: 14.7 us -> none
  transfers between devices with their start and end apart: 5 -> 3, of which waited for: 2 -> 3; matrix products, arithmetic and copies ran while one was open for 31% -> 1% of each run, Pallas kernels for 0% -> 0%
where the time goes in v1:
time: 94.1 us; the launch traced here: 93.5 us
  Pallas kernels  42.1 us (45%)
  waiting for transfers between devices  22.9 us (24%)
  starting transfers between devices  14.7 us (16%)
  local copies, waits for them, and re-layouts  11.5 us (12%)
  other arithmetic  1.35 us (1%)
  between operations  1.01 us (1%)
    all_to_all x2, waiting for transfers between devices, local(): lax.all_to_all(message, 'cell', split_axis=0, concat_axis=0, tiled=True)  15.9 us
    pallas_call x1, Pallas kernels, local(): pl.pallas_call(backward_kernel, grid=grid, in_specs=net_specs + [pl.Block...  14.5 us
    pallas_call x1, Pallas kernels, local(): pl.pallas_call(ray_kernel, out_shape=(jax.ShapeDtypeStruct((4, rows_local...  11.1 us
    all_to_all x2, starting transfers between devices, local(): lax.all_to_all(message, 'cell', split_axis=0, concat_axis=0, tiled=True)  11.1 us
    pallas_call x1, Pallas kernels, local(): pl.pallas_call(forward_kernel, grid=grid, in_specs=net_specs, out_specs=p...  7.56 us
    all_to_all x1, waiting for transfers between devices, local(): lax.all_to_all(outputs, 'cell', split_axis=0, concat_axis=0, tiled=True)  6.96 us
    unnamed x35, local copies, waits for them, and re-layouts  5.16 us
    pallas_call x1, Pallas kernels, local(): pl.pallas_call(table_kernel, grid=(codes_total // block,), in_specs=[pl.B...  4.81 us
  transfers between devices with their start and end apart: 3, of which 3 were waited for; matrix products, arithmetic and copies ran while one was open for 1% of the time, Pallas kernels for 0%

profile of v1, /device:TPU:0, one launch (start us, length us, event | category | flops | bytes accessed | tf_op | source)
XLA Modules:
  0.0 93.5 jit_solution(11368738835111093374)
XLA Ops:
  0.7 0.7 convert_element_type.20
  1.4 0.1 reshape.252
  1.5 0.8 reshape.223
  2.3 0.1 multiply_subtract_fusion
  2.5 0.1 reshape.224
  2.6 0.1 copy.45
  2.7 0.6 copy-done.6
  3.4 4.1 %pick.1 = (f32[3,6144]{1,0:T(4,128)S(1)}, f32[48,64]{1,0:T(8,128)S(1)}) custom-call(s32[1,6144]{1,0:T(1,128)S(1)} %get-tuple-element.42.ray_ref, s32[1,6144]{1,0:T(1,128)S(1)} %get-tuple-element.41.sam_ref, f32[3,96,64]{2,1,0:T(8,128)S(1)} %bitcast.51, s32[1,64]{1,0:T(1,128)S(1)} %bitcast.60, f32[48,2048]{1,0:T(8,128)S(1)} %copy-done.2), custom_call_target="tpu_custom_call" | custom-call | tf_op jit(solution)/shard_map/pick/pallas_call | solution.py:315
  7.6 0.7 copy.48
  8.4 7.5 %all-to-all-start = ((f32[16,1,1504]{2,1,0:T(1,128)}), f32[16,1,1504]{2,1,0:T(1,128)S(1)}, u32[]{:S(2)}, u32[]{:S(2)}) async-start(f32[16,1,1504]{2,1,0:T(1,128)} %copy.48), calls=%async_computation | async-start | bytes 196608 | tf_op jit(solution)/shard_map/all_to_all | solution.py:330
  16.1 0.6 copy-done.11
  16.7 0.1 copy.50
  16.8 0.6 copy-done.9
  17.4 0.1 copy.62.b1_ref
  17.5 0.5 copy-done.10
  18.0 0.1 copy.63.b2_ref
  18.2 5.1 %all-to-all-done = f32[16,1,1504]{2,1,0:T(1,128)S(1)} async-done(((f32[16,1,1504]{2,1,0:T(1,128)}), f32[16,1,1504]{2,1,0:T(1,128)S(1)}, u32[]{:S(2)}, u32[]{:S(2)}) %all-to-all-start) | async-done | bytes 96288 | tf_op jit(solution)/shard_map/all_to_all | solution.py:330
  23.3 0.1 reshape.230
  23.5 0.1 reshape.231
  23.7 0.7 copy-done
  24.5 7.6 %forward.1 = f32[2,4,3072]{2,1,0:T(4,128)S(1)} custom-call(f32[2,3,3072]{2,1,0:T(4,128)S(1)} %copy.61.pos_ref, f32[64,3]{1,0:T(8,128)S(1)} %bitcast.53, bf16[2,128,256]{2,1,0:T(8,128)(2,1)S(1)} %copy-done.1, f32[2,256,1]{2,1,0:T(8,128)S(1)} %copy.62.b1_ref, bf16[2,256,256]{2,1,0:T(8,128)(2,1)S(1)} %copy-done, f32[2,256,1]{2,1,0:T(8,128)S(1)} %copy.63.b2_ref, ...), custom_call_target="tpu_custom_call" | custom-call | tf_op jit(solution)/shard_map/forward/pallas_call | solution.py:360
  32.0 0.1 reshape.233
  32.1 0.1 copy.80
  32.2 0.8 all_to_all.30
  33.1 3.6 %all-to-all-start.1 = ((f32[16,1,1536]{2,1,0:T(1,128)}), f32[16,1,1536]{2,1,0:T(1,128)S(1)}, u32[]{:S(2)}, u32[]{:S(2)}) async-start(f32[16,1,1536]{2,1,0:T(1,128)} %all_to_all.30), calls=%async_computation.1 | async-start | bytes 196608 | tf_op jit(solution)/shard_map/all_to_all | solution.py:371
  36.8 0.1 reshape.253.live_ref
  36.9 0.1 reshape.232.cell_ref
  37.0 0.1 reshape.236
  37.2 7.0 %all-to-all-done.1 = f32[16,1,1536]{2,1,0:T(1,128)S(1)} async-done(((f32[16,1,1536]{2,1,0:T(1,128)}), f32[16,1,1536]{2,1,0:T(1,128)S(1)}, u32[]{:S(2)}, u32[]{:S(2)}) %all-to-all-start.1) | async-done | bytes 98336 | tf_op jit(solution)/shard_map/all_to_all | solution.py:371
  44.1 0.2 reduce
  44.4 0.7 copy-done.5
  45.1 11.1 %rays.1 = (f32[4,6144]{1,0:T(4,128)S(1)}, f32[96,48]{1,0:T(8,128)S(1)}, f32[48,64]{1,0:T(8,128)S(1)}) custom-call(s32[1,6144]{1,0:T(1,128)S(1)} %get-tuple-element.42.ray_ref, s32[1,6144]{1,0:T(1,128)S(1)} %get-tuple-element.41.sam_ref, s32[1,6144]{1,0:T(1,128)S(1)} %reshape.232.cell_ref, f32[1,6144]{1,0:T(1,128)S(1)} %reshape.253.live_ref, ...), custom_call_target="tpu_custom_call" | custom-call | tf_op jit(solution)/shard_map/rays/pallas_call | solution.py:375
  56.4 0.1 reshape.242
  56.5 0.1 concatenate.11
  56.6 0.9 %all_to_all.27 = f32[16,1,4896]{2,1,0:T(1,128)} reshape(f32[16,4896]{1,0:T(8,128)S(1)} %concatenate.11) | data formatting | bytes 626688 | tf_op jit(solution)/shard_map/all_to_all | solution.py:412
  57.6 3.5 %all-to-all-start.2 = ((f32[16,1,4896]{2,1,0:T(1,128)}), f32[16,1,4896]{2,1,0:T(1,128)S(1)}, u32[]{:S(2)}, u32[]{:S(2)}) async-start(f32[16,1,4896]{2,1,0:T(1,128)} %all_to_all.27), calls=%async_computation.2 | async-start | bytes 638976 | tf_op jit(solution)/shard_map/all_to_all | solution.py:412
  61.3 10.8 %all-to-all-done.2 = f32[16,1,4896]{2,1,0:T(1,128)S(1)} async-done(((f32[16,1,4896]{2,1,0:T(1,128)}), f32[16,1,4896]{2,1,0:T(1,128)S(1)}, u32[]{:S(2)}, u32[]{:S(2)}) %all-to-all-start.2) | async-done | bytes 313376 | tf_op jit(solution)/shard_map/all_to_all | solution.py:412
  72.1 0.1 slice.29
  72.2 0.1 reshape.247
  72.3 0.6 copy.65
  72.9 0.1 reshape.243
  73.1 0.1 reshape.244.slope_ref
  73.2 14.5 %backward.1 = (f32[2,128,256]{2,1,0:T(8,128)}, f32[2,1,256]{2,1,0:T(1,128)S(1)}, f32[2,256,256]{2,1,0:T(8,128)}, f32[2,1,256]{2,1,0:T(1,128)S(1)}, f32[2,4,256]{2,1,0:T(4,128)}) custom-call(f32[2,3,3072]{2,1,0:T(4,128)S(1)} %copy.61.pos_ref, f32[64,3]{1,0:T(8,128)S(1)} %bitcast.54, bf16[2,128,256]{2,1,0:T(8,128)(2,1)S(1)} %copy-done.1, ...), custom_call_target="tpu_custom_call" | custom-call | tf_op jit(solution)/shard_map/backward/pallas_call | solution.py:421
  87.7 0.1 reshape.249
  87.8 0.1 copy.64
  88.0 0.2 reshape.250.terms_ref
  88.1 0.6 copy_bitcast_fusion.5
  88.7 4.8 %table.1 = f32[48,2048]{1,0:T(8,128)} custom-call(s32[1,1024]{1,0:T(1,128)S(1)} %reshape.248.codes_ref, f32[48,1024]{1,0:T(8,128)S(1)} %reshape.250.terms_ref), custom_call_target="tpu_custom_call" | custom-call | tf_op jit(solution)/shard_map/table/pallas_call | solution.py:444
  (47 shorter events, 0.9 us)
Async XLA Ops:
  0.6 0.7 copy-start.12
  0.6 1.8 %copy-start.7 = (f32[3,6144]{1,0:T(4,128)S(1)}, f32[3,6144]{1,0:T(4,128)}, u32[]{:S(2)}) copy-start(f32[3,6144]{1,0:T(4,128)} %param.15) | copy-start | bytes 221188
  0.7 2.1 %copy-start.2 = (f32[48,2048]{1,0:T(8,128)S(1)}, f32[48,2048]{1,0:T(8,128)}, u32[]{:S(2)}) copy-start(f32[48,2048]{1,0:T(8,128)} %table_ref.1) | copy-start | bytes 1179652
  2.7 0.7 copy-start.6
  8.4 7.5 %copy-start.8 = (f32[6144]{0:T(1024)S(1)}, f32[6144]{0:T(1024)}, u32[]{:S(2)}) copy-start(f32[6144]{0:T(1024)} %param.16) | copy-start | bytes 73732
  8.4 14.9 %all-to-all-start = ((f32[16,1,1504]{2,1,0:T(1,128)}), f32[16,1,1504]{2,1,0:T(1,128)S(1)}, u32[]{:S(2)}, u32[]{:S(2)}) async-start(f32[16,1,1504]{2,1,0:T(1,128)} %copy.48), calls=%async_computation | async-start | bytes 196608 | tf_op jit(solution)/shard_map/all_to_all | solution.py:330
  16.0 0.7 copy-start.11
  16.7 0.7 copy-start.9
  17.4 0.7 copy-start.10
  23.5 1.0 %copy-start = (bf16[2,256,256]{2,1,0:T(8,128)(2,1)S(1)}, bf16[2,256,256]{2,1,0:T(8,128)(2,1)}, u32[]{:S(2)}) copy-start(bf16[2,256,256]{2,1,0:T(8,128)(2,1)} %w2_ref.3) | copy-start | bytes 786436
  23.5 1.0 %copy-start.1 = (bf16[2,128,256]{2,1,0:T(8,128)(2,1)S(1)}, bf16[2,128,256]{2,1,0:T(8,128)(2,1)}, u32[]{:S(2)}) copy-start(bf16[2,128,256]{2,1,0:T(8,128)(2,1)} %w1_ref.3) | copy-start | bytes 393220
  23.6 0.8 copy-start.3
  33.1 3.7 %copy-start.13 = (s32[32]{0:T(128)S(1)}, s32[32]{0:T(128)}, u32[]{:S(2)}) copy-start(s32[32]{0:T(128)} %param.29) | copy-start | bytes 388
  33.1 11.0 %all-to-all-start.1 = ((f32[16,1,1536]{2,1,0:T(1,128)}), f32[16,1,1536]{2,1,0:T(1,128)S(1)}, u32[]{:S(2)}, u32[]{:S(2)}) async-start(f32[16,1,1536]{2,1,0:T(1,128)} %all_to_all.30), calls=%async_computation.1 | async-start | bytes 196608 | tf_op jit(solution)/shard_map/all_to_all | solution.py:371
  44.4 0.7 copy-start.5
  44.4 0.7 copy-start.4
  57.6 14.5 %all-to-all-start.2 = ((f32[16,1,4896]{2,1,0:T(1,128)}), f32[16,1,4896]{2,1,0:T(1,128)S(1)}, u32[]{:S(2)}, u32[]{:S(2)}) async-start(f32[16,1,4896]{2,1,0:T(1,128)} %all_to_all.27), calls=%async_computation.2 | async-start | bytes 638976 | tf_op jit(solution)/shard_map/all_to_all | solution.py:412

commit v2 on v1

v2 whole, which is shorter than its diff:
```python
import functools

import jax
import jax.numpy as jnp
from jax import lax
from jax.experimental import pallas as pl
from jax.experimental.pallas import tpu as pltpu
from jax.sharding import PartitionSpec as P

loss_scale = 256.0
F32 = jnp.float32
BF16 = jnp.bfloat16
HIGH = lax.Precision.HIGHEST
MESH = pl.DeviceIdType.MESH


def nn(a, b, precision=None):
    return lax.dot_general(
        a, b, (((1,), (0,)), ((), ())), precision=precision, preferred_element_type=F32
    )


def nt(a, b, precision=None):
    return lax.dot_general(
        a, b, (((1,), (1,)), ((), ())), precision=precision, preferred_element_type=F32
    )


def tn(a, b, precision=None):
    return lax.dot_general(
        a, b, (((0,), (0,)), ((), ())), precision=precision, preferred_element_type=F32
    )


def chunk_of(total, most):
    best = total
    for size in range(128, most + 1, 128):
        if total % size == 0:
            best = size
    return best


def split3(value):
    high = value.astype(BF16)
    rest = value - high.astype(F32)
    mid = rest.astype(BF16)
    low = (rest - mid.astype(F32)).astype(BF16)
    return high, mid, low


def one_hot(index_row, depth):
    rows = lax.broadcasted_iota(jnp.int32, (depth, index_row.shape[1]), 0)
    return rows == index_row


def hot_bf16(mask):
    return jnp.where(mask, 1.0, 0.0).astype(BF16)


def sigmoid(value):
    return 0.5 * jnp.tanh(0.5 * value) + 0.5


PI_A = 3.140625
PI_B = 9.676535897932e-4


def sine(angle, shift):
    turns = jnp.round(angle * 0.3183098861837907 + shift)
    whole = turns - shift
    rest = (angle - whole * PI_A) - whole * PI_B
    odd = turns - 2.0 * jnp.floor(turns * 0.5)
    rest = rest * (1.0 - 2.0 * odd)
    square = rest * rest
    poly = -2.5052108e-8
    poly = poly * square + 2.7557319e-6
    poly = poly * square - 1.9841270e-4
    poly = poly * square + 8.3333333e-3
    poly = poly * square - 1.6666667e-1
    return rest + rest * square * poly


def start_all(me, owners, source, landing, send_sems, recv_sems):
    def start(step, carry):
        there = lax.rem(me + step, owners)
        pltpu.make_async_remote_copy(
            src_ref=source(there),
            dst_ref=landing.at[me],
            send_sem=send_sems.at[step],
            recv_sem=recv_sems.at[me],
            device_id={"cell": there},
            device_id_type=MESH,
        ).start()
        return carry

    lax.fori_loop(1, owners, start, 0)


def wait_all(me, owners, source, landing, send_sems, recv_sems):
    def wait(step, carry):
        there = lax.rem(me + step, owners)
        copy = pltpu.make_async_remote_copy(
            src_ref=source(there),
            dst_ref=landing.at[there],
            send_sem=send_sems.at[step],
            recv_sem=recv_sems.at[there],
            device_id={"cell": there},
            device_id_type=MESH,
        )
        copy.wait_recv()
        copy.wait_send()
        return carry

    lax.fori_loop(1, owners, wait, 0)


def encode_block(pos, freq):
    angle = pos[0:1] * freq[:, 0:1] + pos[1:2] * freq[:, 1:2]
    angle = angle + pos[2:3] * freq[:, 2:3]
    return jnp.concatenate([sine(angle, 0.0), sine(angle, 0.5)], axis=0).astype(BF16)


def whole_kernel(
    owners,
    capacity,
    ray_ref,
    sam_ref,
    cell_ref,
    live_ref,
    pos_ref,
    codes_ref,
    table_ref,
    extra_ref,
    freq_ref,
    w1_ref,
    b1_ref,
    w2_ref,
    b2_ref,
    head_ref,
    deltas_ref,
    back_ref,
    target_ref,
    gw1_ref,
    gb1_ref,
    gw2_ref,
    gb2_ref,
    gh_ref,
    ga_ref,
    gt_ref,
    extra_land,
    pos_send,
    pos_land,
    out_send,
    out_land,
    slope_send,
    slope_land,
    term_send,
    term_land,
    slot_ref,
    cellpos_ref,
    enc_ref,
    act1_ref,
    act2_ref,
    d1_ref,
    d2_ref,
    cellout_ref,
    cellslope_ref,
    outs_ref,
    slope_ref,
    heads_ref,
    app_ref,
    partial_ref,
    shift_ref,
    rows_ref,
    sums_ref,
    send_sems,
    recv_sems,
):
    me = lax.axis_index("cell")
    barrier = pltpu.get_barrier_semaphore()

    def greet(step, carry):
        pl.semaphore_signal(
            barrier,
            inc=1,
            device_id={"cell": lax.rem(me + step, owners)},
            device_id_type=MESH,
        )
        return carry

    lax.fori_loop(1, owners, greet, 0)

    samples, rays = deltas_ref.shape
    slots = ray_ref.shape[1]
    cells = heads_ref.shape[0] // 3
    cell_dev = w1_ref.shape[0]
    app_width = app_ref.shape[0]
    codes_total = table_ref.shape[1]
    per_owner = cell_dev * capacity
    chunk = chunk_of(slots, 1024)
    steps = slots // chunk

    parts = split3(pos_ref[...].reshape(3 * samples, rays))
    code_hot = hot_bf16(one_hot(codes_ref[...], codes_total))
    table_parts = split3(table_ref[...])
    app_ref[...] = (nn(table_parts[2], code_hot) + nn(table_parts[1], code_hot)) + nn(
        table_parts[0], code_hot
    )

    def pick_rows(step, carry):
        here = pl.ds(pl.multiple_of(step * chunk, 128), chunk)
        ray_hot = hot_bf16(one_hot(ray_ref[:, here], rays))
        sam_hot = one_hot(sam_ref[:, here], samples)
        picked = (nn(parts[2], ray_hot) + nn(parts[1], ray_hot)) + nn(parts[0], ray_hot)
        for axis in range(3):
            part = picked[axis * samples : (axis + 1) * samples]
            slot_ref[axis : axis + 1, here] = jnp.sum(
                jnp.where(sam_hot, part, 0.0), axis=0, keepdims=True
            )
        return carry

    lax.fori_loop(0, steps, pick_rows, 0)
    for n in range(owners):
        pos_send[n] = slot_ref[:, n * per_owner : (n + 1) * per_owner]
    pl.semaphore_wait(barrier, owners - 1)
    pos_args = (me, owners, lambda n: pos_send.at[n], pos_land, send_sems.at[0], recv_sems.at[0])
    start_all(*pos_args)
    extra_args = (me, owners, lambda n: extra_ref, extra_land, send_sems.at[1], recv_sems.at[1])
    start_all(*extra_args)
    pos_land[me] = pos_send[me]
    extra_land[me] = extra_ref[...]
    wait_all(*pos_args)
    for j in range(cell_dev):
        cellpos_ref[j] = jnp.concatenate(
            [pos_land[n][:, j * capacity : (j + 1) * capacity] for n in range(owners)], axis=1
        )

    slots_cell = owners * capacity
    lanes = chunk_of(slots_cell, 1024)
    blocks = slots_cell // lanes

    def forward(step, carry):
        j = step // blocks
        here = pl.ds(pl.multiple_of((step % blocks) * lanes, 128), lanes)
        encoded = encode_block(cellpos_ref[j, :, here], freq_ref[...])
        enc_ref[j, :, here] = encoded
        pre = tn(w1_ref[j], encoded) + b1_ref[j]
        sig = sigmoid(pre)
        act = pre * sig
        d1_ref[j, :, here] = sig + act * (1.0 - sig)
        act = act.astype(BF16)
        act1_ref[j, :, here] = act
        pre = tn(w2_ref[j], act) + b2_ref[j]
        sig = sigmoid(pre)
        act = pre * sig
        d2_ref[j, :, here] = sig + act * (1.0 - sig)
        act = act.astype(BF16)
        act2_ref[j, :, here] = act
        cellout_ref[j, :, here] = nn(head_ref[j], act)
        return carry

    lax.fori_loop(0, cell_dev * blocks, forward, 0)
    outs = [cellout_ref[j] for j in range(cell_dev)]
    for n in range(owners):
        out_send[n] = jnp.concatenate(
            [part[:, n * capacity : (n + 1) * capacity] for part in outs], axis=1
        )
    out_args = (me, owners, lambda n: out_send.at[n], out_land, send_sems.at[2], recv_sems.at[2])
    start_all(*out_args)
    out_land[me] = out_send[me]

    wait_all(*extra_args)

    def place_heads(n, carry):
        for k in range(3):
            heads_ref[pl.ds(k * cells + n * cell_dev, cell_dev), :] = extra_land[
                n, k * cell_dev : (k + 1) * cell_dev, :app_width
            ]
        return carry

    lax.fori_loop(0, owners, place_heads, 0)
    shift_ref[...] = nn(heads_ref[...], app_ref[...], HIGH)
    rows_ref[...] = jnp.zeros_like(rows_ref)
    shift_parts = split3(shift_ref[...])
    wait_all(*out_args)
    for n in range(owners):
        outs_ref[:, n * per_owner : (n + 1) * per_owner] = out_land[n]

    def gather_rows(step, carry):
        here = pl.ds(pl.multiple_of(step * chunk, 128), chunk)
        ray_hot = hot_bf16(one_hot(ray_ref[:, here], rays))
        sam_hot = one_hot(sam_ref[:, here], samples)
        cell_hot = one_hot(cell_ref[:, here], cells)
        shifts = (nn(shift_parts[2], ray_hot) + nn(shift_parts[1], ray_hot)) + nn(
            shift_parts[0], ray_hot
        )
        columns = [outs_ref[0:1, here]]
        for k in range(3):
            part = shifts[k * cells : (k + 1) * cells]
            picked = jnp.sum(jnp.where(cell_hot, part, 0.0), axis=0, keepdims=True)
            columns.append(outs_ref[k + 1 : k + 2, here] + picked)
        columns.append(live_ref[:, here])
        spread = [jnp.where(sam_hot, column, 0.0).astype(BF16) for column in columns]
        rows_ref[...] += nt(jnp.concatenate(spread, axis=0), ray_hot)
        return carry

    lax.fori_loop(0, steps, gather_rows, 0)
    raw = [rows_ref[k * samples : (k + 1) * samples] for k in range(4)]
    routed = rows_ref[4 * samples : 5 * samples]
    deltas = deltas_ref[...]
    first = lax.broadcasted_iota(jnp.int32, (samples, samples), 0)
    second = lax.broadcasted_iota(jnp.int32, (samples, samples), 1)
    earlier = jnp.where(second < first, 1.0, 0.0)
    later = jnp.where(second > first, 1.0, 0.0)
    tail = jnp.exp(-jnp.abs(raw[0]))
    softplus = jnp.maximum(raw[0], 0.0) + jnp.log1p(tail)
    optical = routed * softplus * deltas
    before = nn(earlier, optical, HIGH)
    total = jnp.sum(optical, axis=0, keepdims=True)
    through = jnp.exp(-before)
    kept = jnp.exp(-optical)
    weight = through * (1.0 - kept)
    leaving = jnp.exp(-total)
    back_slope = jnp.zeros_like(total)
    weight_slope = jnp.zeros_like(weight)
    slope_parts = []
    for k in range(3):
        color = jax.nn.sigmoid(raw[k + 1])
        pixel = jnp.sum(weight * color, axis=0, keepdims=True) + leaving * back_ref[k : k + 1]
        pixel_slope = loss_scale * (pixel - target_ref[k : k + 1])
        back_slope = back_slope + pixel_slope * back_ref[k : k + 1]
        weight_slope = weight_slope + pixel_slope * color
        slope_parts.append((weight * pixel_slope * (color * (1.0 - color))).astype(BF16))
    after = nn(later, weight_slope * weight, HIGH)
    optical_slope = weight_slope * through * kept - after - leaving * back_slope
    density_slope = optical_slope * deltas * routed * jax.nn.sigmoid(raw[0])
    stacked = jnp.concatenate([density_slope.astype(BF16)] + slope_parts, axis=0)
    sums_ref[...] = jnp.zeros_like(sums_ref)

    def spread_slopes(step, carry):
        here = pl.ds(pl.multiple_of(step * chunk, 128), chunk)
        ray_hot = hot_bf16(one_hot(ray_ref[:, here], rays))
        sam_hot = one_hot(sam_ref[:, here], samples)
        cell_hot = one_hot(cell_ref[:, here], cells)
        picked = nn(stacked, ray_hot)
        spread = []
        for k in range(4):
            part = picked[k * samples : (k + 1) * samples]
            column = jnp.sum(jnp.where(sam_hot, part, 0.0), axis=0, keepdims=True)
            slope_ref[k : k + 1, here] = column
            if k:
                spread.append(jnp.where(cell_hot, column, 0.0).astype(BF16))
        sums_ref[...] += nt(jnp.concatenate(spread, axis=0), ray_hot)
        return carry

    lax.fori_loop(0, steps, spread_slopes, 0)
    for n in range(owners):
        slope_send[n] = slope_ref[:, n * per_owner : (n + 1) * per_owner]
    slope_args = (
        me,
        owners,
        lambda n: slope_send.at[n],
        slope_land,
        send_sems.at[3],
        recv_sems.at[3],
    )
    start_all(*slope_args)
    slope_land[me] = slope_send[me]
    sums = sums_ref[...]
    partial_ref[...] = nt(sums, app_ref[...], HIGH)
    terms = tn(heads_ref[...], sums, HIGH)

    def place_terms(n, carry):
        term_send[n, :app_width, :rays] = terms
        for k in range(3):
            term_send[
                n, app_width + k * cell_dev : app_width + (k + 1) * cell_dev, :app_width
            ] = partial_ref[pl.ds(k * cells + n * cell_dev, cell_dev), :]
        return carry

    term_send[...] = jnp.zeros_like(term_send)
    lax.fori_loop(0, owners, place_terms, 0)
    term_args = (
        me,
        owners,
        lambda n: term_send.at[n],
        term_land,
        send_sems.at[4],
        recv_sems.at[4],
    )
    wait_all(*slope_args)
    start_all(*term_args)
    term_land[me] = term_send[me]
    for j in range(cell_dev):
        cellslope_ref[j] = jnp.concatenate(
            [slope_land[n][:, j * capacity : (j + 1) * capacity] for n in range(owners)], axis=1
        )

    for ref in (gw1_ref, gb1_ref, gw2_ref, gb2_ref, gh_ref):
        ref[...] = jnp.zeros_like(ref)

    def backward(step, carry):
        j = step // blocks
        here = pl.ds(pl.multiple_of((step % blocks) * lanes, 128), lanes)
        slopes = cellslope_ref[j, :, here].astype(BF16)
        ones = jnp.ones((8, lanes), BF16)
        gh_ref[j] += nt(slopes, act2_ref[j, :, here])
        delta = (tn(head_ref[j], slopes) * d2_ref[j, :, here]).astype(BF16)
        gw2_ref[j] += nt(act1_ref[j, :, here], delta)
        gb2_ref[j] += nt(ones, delta)[0:1]
        delta = (nn(w2_ref[j], delta) * d1_ref[j, :, here]).astype(BF16)
        gw1_ref[j] += nt(enc_ref[j, :, here], delta)
        gb1_ref[j] += nt(ones, delta)[0:1]
        return carry

    lax.fori_loop(0, cell_dev * blocks, backward, 0)

    wait_all(*term_args)
    total = term_land[0]
    for n in range(1, owners):
        total = total + term_land[n]
    ga_ref[...] = total[app_width:, :app_width]
    terms = jnp.concatenate([term_land[n][:app_width, :rays] for n in range(owners)], axis=1)
    code_row = 3 * cell_dev
    all_codes = jnp.concatenate(
        [extra_land[n][code_row : code_row + 1, :rays] for n in range(owners)], axis=1
    ).astype(jnp.int32)
    term_parts = split3(terms)
    block = chunk_of(codes_total, 512)
    for first_code in range(0, codes_total, block):
        hot = hot_bf16(one_hot(all_codes - first_code, block))
        gt_ref[:, first_code : first_code + block] = (
            nt(term_parts[2], hot) + nt(term_parts[1], hot)
        ) + nt(term_parts[0], hot)


def local(
    positions,
    deltas,
    background,
    target,
    ray_codes,
    frequencies,
    w_first,
    b_first,
    w_second,
    b_second,
    head_out,
    head_app,
    app_table,
    dispatch,
    counts,
):
    owners = lax.axis_size("cell")
    lists, capacity = dispatch.shape
    cell_dev, encoding, width = w_first.shape
    rows_local = positions.shape[1]
    rays = ray_codes.shape[0]
    samples = rows_local // rays
    app_width, codes_total = app_table.shape
    slots_cell = owners * capacity

    listed = dispatch.reshape(1, rows_local)
    slot_ray = listed // samples
    slot_sam = listed - slot_ray * samples
    slot_cell = lax.broadcasted_iota(jnp.int32, (lists, capacity), 0).reshape(1, rows_local)
    live = (jnp.arange(capacity, dtype=jnp.int32)[None, :] < counts[:, None]).astype(F32)
    live = live.reshape(1, rows_local)
    pos_grid = jnp.transpose(positions.reshape(3, rays, samples), (0, 2, 1))
    delta_grid = deltas.reshape(rays, samples).T

    per_owner = cell_dev * capacity
    side = max(rays, app_width)
    extra = jnp.transpose(head_app.astype(F32), (1, 0, 2)).reshape(3 * cell_dev, app_width)
    extra = jnp.concatenate(
        [
            jnp.pad(extra, ((0, 0), (0, side - app_width))),
            jnp.pad(ray_codes.astype(F32)[None, :], ((0, 0), (0, side - rays))),
        ],
        axis=0,
    )
    term_rows = app_width + 3 * cell_dev
    in_vmem = pl.BlockSpec(memory_space=pltpu.VMEM)
    outs = (
        jax.ShapeDtypeStruct((cell_dev, encoding, width), F32),
        jax.ShapeDtypeStruct((cell_dev, 1, width), F32),
        jax.ShapeDtypeStruct((cell_dev, width, width), F32),
        jax.ShapeDtypeStruct((cell_dev, 1, width), F32),
        jax.ShapeDtypeStruct((cell_dev, 4, width), F32),
        jax.ShapeDtypeStruct((3 * cell_dev, app_width), F32),
        jax.ShapeDtypeStruct((app_width, codes_total), F32),
    )
    (
        grad_w_first,
        grad_b_first,
        grad_w_second,
        grad_b_second,
        grad_head_out,
        grad_head_app,
        grad_table,
    ) = pl.pallas_call(
        functools.partial(whole_kernel, owners, capacity),
        out_shape=outs,
        in_specs=[in_vmem] * 17,
        out_specs=(in_vmem,) * 7,
        scratch_shapes=[
            pltpu.VMEM((owners,) + extra.shape, F32),
            pltpu.VMEM((owners, 3, per_owner), F32),
            pltpu.VMEM((owners, 3, per_owner), F32),
            pltpu.VMEM((owners, 4, per_owner), F32),
            pltpu.VMEM((owners, 4, per_owner), F32),
            pltpu.VMEM((owners, 4, per_owner), F32),
            pltpu.VMEM((owners, 4, per_owner), F32),
            pltpu.VMEM((owners, term_rows, side), F32),
            pltpu.VMEM((owners, term_rows, side), F32),
            pltpu.VMEM((3, rows_local), F32),
            pltpu.VMEM((cell_dev, 3, slots_cell), F32),
            pltpu.VMEM((cell_dev, encoding, slots_cell), BF16),
            pltpu.VMEM((cell_dev, width, slots_cell), BF16),
            pltpu.VMEM((cell_dev, width, slots_cell), BF16),
            pltpu.VMEM((cell_dev, width, slots_cell), F32),
            pltpu.VMEM((cell_dev, width, slots_cell), F32),
            pltpu.VMEM((cell_dev, 4, slots_cell), F32),
            pltpu.VMEM((cell_dev, 4, slots_cell), F32),
            pltpu.VMEM((4, rows_local), F32),
            pltpu.VMEM((4, rows_local), F32),
            pltpu.VMEM((3 * lists, app_width), F32),
            pltpu.VMEM((app_width, rays), F32),
            pltpu.VMEM((3 * lists, app_width), F32),
            pltpu.VMEM((3 * lists, rays), F32),
            pltpu.VMEM((5 * samples, rays), F32),
            pltpu.VMEM((3 * lists, rays), F32),
            pltpu.SemaphoreType.DMA((5, owners)),
            pltpu.SemaphoreType.DMA((5, owners)),
        ],
        compiler_params=pltpu.CompilerParams(
            vmem_limit_bytes=56 * 1024 * 1024, collective_id=0, has_side_effects=True
        ),
        name="whole",
    )(
        slot_ray,
        slot_sam,
        slot_cell,
        live,
        pos_grid,
        ray_codes.reshape(1, rays),
        app_table,
        extra,
        frequencies.T,
        w_first,
        b_first[:, :, None],
        w_second,
        b_second[:, :, None],
        head_out,
        delta_grid,
        background,
        target,
    )
    grad_head_app = jnp.transpose(grad_head_app.reshape(3, cell_dev, app_width), (1, 0, 2))
    return (
        grad_w_first,
        grad_b_first.reshape(cell_dev, width),
        grad_w_second,
        grad_b_second.reshape(cell_dev, width),
        grad_head_out,
        grad_head_app,
        grad_table,
    )


def solution(mesh):
    placed = (
        P(None, ("groups", "cell")),
        P(("groups", "cell")),
        P(None, ("groups", "cell")),
        P(None, ("groups", "cell")),
        P(("groups", "cell")),
        P(),
        P("cell", None, None),
        P("cell", None),
        P("cell", None, None),
        P("cell", None),
        P("cell", None, None),
        P("cell", None, None),
        P(),
        P(("groups", "cell"), None),
        P(("groups", "cell")),
    )
    return jax.shard_map(
        local,
        mesh=mesh,
        in_specs=placed,
        out_specs=(
            P(("groups", "cell"), None, None),
            P(("groups", "cell"), None),
            P(("groups", "cell"), None, None),
            P(("groups", "cell"), None),
            P(("groups", "cell"), None, None),
            P(("groups", "cell"), None, None),
            P("groups", None),
        ),
        check_vma=False,
    )
```

time: 94.1 us -> 70.7 us (0.75)
  the two profiles are of different devices: /device:TPU:0 before, /device:TPU:13 now
where the time goes in v2:
time: 70.7 us; the launch traced here: 70.4 us
  Pallas kernels  54.8 us (78%)
  local copies, waits for them, and re-layouts  13.5 us (19%)
  other arithmetic  1.46 us (2%)
    pallas_call x1, Pallas kernels, local(): pl.pallas_call(functools.partial(whole_kernel, owners, capacity), out_sha...  54.8 us
    unnamed x28, local copies, waits for them, and re-layouts  6.5 us

profile of v2, /device:TPU:13, one launch (start us, length us, event | category | flops | bytes accessed | tf_op | source)
XLA Modules:
  0.0 70.4 jit_solution(5725451250376417391)
XLA Ops:
  0.6 0.0 copy-start.10
  0.6 0.0 copy-start.8
  0.7 0.6 copy-done.10
  1.3 0.0 copy-done.8
  1.4 0.6 pad_maximum_fusion.extra_ref
  2.0 0.8 %reshape.155 = s32[1,6144]{1,0:T(1,128)S(1)} reshape(s32[32,192]{1,0:T(8,128)} %param.28) | data formatting | bytes 49152 | tf_op jit(solution)/shard_map/reshape | solution.py:463
  2.8 0.0 copy-start.3
  2.8 0.8 %multiply_subtract_fusion = (s32[1,6144]{1,0:T(1,128)}, s32[1,6144]{1,0:T(1,128)}) fusion(s32[1,6144]{1,0:T(1,128)S(1)} %reshape.155), kind=kLoop, calls=%fused_computation.3 | loop fusion | flops 61440 | bytes 73728 | tf_op jit(solution)/shard_map/sub | solution.py:465
  3.6 0.0 copy-done.3
  3.6 0.1 reshape.160
  3.7 0.0 copy-start.7
  3.7 0.7 %copy.25 = f32[64,96]{0,1:T(8,128)} copy(f32[64,96]{1,0:T(8,128)S(1)} %reshape.160) | data formatting | bytes 49152 | tf_op jit(solution)/shard_map/reshape | solution.py:470
  4.4 0.0 copy-done.7
  4.4 0.0 copy-start.9
  4.4 0.7 %copy.24 = f32[3,64]{0,1:T(8,128)} copy(f32[3,64]{1,0:T(4,128)S(1)} %copy-done.7) | data formatting | bytes 1536 | tf_op args[5]
  5.1 0.0 copy-start.2
  5.1 0.0 copy-done.9
  5.1 0.1 fusion
  5.2 0.7 reshape.164.live_ref
  5.9 0.7 reshape.156.cell_ref
  6.6 0.0 copy-done.2
  6.6 0.1 reshape.157
  6.7 0.0 copy-start.5
  6.7 0.8 %copy.23 = f32[3,64,96]{1,2,0:T(8,128)} copy(f32[3,64,96]{2,1,0:T(8,128)S(1)} %reshape.157) | data formatting | bytes 147456 | tf_op jit(solution)/shard_map/reshape | solution.py:469
  7.5 0.0 copy-done.5
  7.5 0.0 copy-start.6
  7.5 0.9 %copy.26.b1_ref = f32[2,256,1]{2,1,0:T(8,128)} copy(f32[2,256,1]{1,0,2:T(2,128)S(1)} %bitcast.18) | data formatting | bytes 4096 | tf_op jit(solution)/shard_map/broadcast_in_dim | solution.py:551
  8.3 0.0 copy-done.6
  8.3 0.9 %copy.27.b2_ref = f32[2,256,1]{2,1,0:T(8,128)} copy(f32[2,256,1]{1,0,2:T(2,128)S(1)} %bitcast.19) | data formatting | bytes 4096 | tf_op jit(solution)/shard_map/broadcast_in_dim | solution.py:553
  9.2 54.8 %whole.1 = (f32[2,128,256]{2,1,0:T(8,128)}, f32[2,1,256]{2,1,0:T(1,128)}, f32[2,256,256]{2,1,0:T(8,128)}, f32[2,1,256]{2,1,0:T(1,128)}, f32[2,4,256]{2,1,0:T(4,1...) custom-call(s32[1,6144]{1,0:T(1,128)} %get-tuple-element.22.ray_ref, s32[1,6144]{1,0:T(1,128)} %get-tuple-element.21.sam_ref, ...), custom_call_target="tpu_custom_call" | custom-call | tf_op jit(solution)/shard_map/whole/pallas_call | solution.py:501
  64.0 0.0 copy-start
  64.0 1.3 %reshape.163 = f32[3,2,48]{2,1,0:T(2,128)} reshape(f32[6,48]{1,0:T(8,128)} %get-tuple-element.19) | data formatting | bytes 2304 | tf_op jit(solution)/shard_map/reshape | solution.py:559
  65.3 1.3 %copy_bitcast_fusion = (f32[2,256]{1,0:T(2,128)}, f32[2,256]{1,0:T(2,128)}) fusion(f32[2,1,256]{2,1,0:T(1,128)} %get-tuple-element.17, f32[2,1,256]{2,1,0:T(1,128)} %get-tuple-element.15), kind=kLoop, calls=%fused_computation.5 | loop fusion | bytes 8192
  66.6 1.7 %copy.36 = f32[2,128,256]{2,1,0:T(8,128)} copy(f32[2,128,256]{2,1,0:T(8,128)} %get-tuple-element.32) | data formatting | bytes 524288
  68.2 0.0 copy-done
  68.2 0.0 copy-start.4
  68.2 0.0 copy-start.1
  68.2 0.8 %copy.37 = f32[2,256,256]{2,1,0:T(8,128)} copy(f32[2,256,256]{2,1,0:T(8,128)S(1)} %copy-done) | data formatting | bytes 1048576
  69.0 0.0 copy-done.4
  69.0 0.6 copy.38
  69.6 0.0 copy-done.1
  69.6 0.7 %copy.39 = f32[48,2048]{1,0:T(8,128)} copy(f32[48,2048]{1,0:T(8,128)S(1)} %copy-done.1) | data formatting | bytes 786432
  (4 shorter events, 0.0 us)
Async XLA Ops:
  0.6 0.7 copy-start.10
  0.6 0.7 copy-start.8
  2.8 0.8 %copy-start.3 = (f32[6144]{0:T(1024)S(1)}, f32[6144]{0:T(1024)}, u32[]{:S(2)}) copy-start(f32[6144]{0:T(1024)} %param.16) | copy-start | bytes 73732
  3.7 0.7 %copy-start.7 = (f32[3,64]{1,0:T(4,128)S(1)}, f32[3,64]{1,0:T(4,128)}, u32[]{:S(2)}) copy-start(f32[3,64]{1,0:T(4,128)} %param.20) | copy-start | bytes 2308
  4.4 0.7 %copy-start.9 = (s32[32]{0:T(128)S(1)}, s32[32]{0:T(128)}, u32[]{:S(2)}) copy-start(s32[32]{0:T(128)} %param.29) | copy-start | bytes 388
  5.1 1.5 %copy-start.2 = (f32[3,6144]{1,0:T(4,128)S(1)}, f32[3,6144]{1,0:T(4,128)}, u32[]{:S(2)}) copy-start(f32[3,6144]{1,0:T(4,128)} %param.15) | copy-start | bytes 221188
  6.7 0.8 %copy-start.5 = (f32[2,256]{1,0:T(2,128)S(1)}, f32[2,256]{1,0:T(2,128)}, u32[]{:S(2)}) copy-start(f32[2,256]{1,0:T(2,128)} %param.22) | copy-start | bytes 6148
  7.5 0.9 %copy-start.6 = (f32[2,256]{1,0:T(2,128)S(1)}, f32[2,256]{1,0:T(2,128)}, u32[]{:S(2)}) copy-start(f32[2,256]{1,0:T(2,128)} %param.24) | copy-start | bytes 6148
  64.0 4.3 %copy-start = (f32[2,256,256]{2,1,0:T(8,128)S(1)}, f32[2,256,256]{2,1,0:T(8,128)}, u32[]{:S(2)}) copy-start(f32[2,256,256]{2,1,0:T(8,128)} %get-tuple-element.34) | copy-start | bytes 1572868
  68.2 0.8 %copy-start.4 = (f32[2,4,256]{2,1,0:T(4,128)S(1)}, f32[2,4,256]{2,1,0:T(4,128)}, u32[]{:S(2)}) copy-start(f32[2,4,256]{2,1,0:T(4,128)} %get-tuple-element.36) | copy-start | bytes 24580
  68.2 1.4 %copy-start.1 = (f32[48,2048]{1,0:T(8,128)S(1)}, f32[48,2048]{1,0:T(8,128)}, u32[]{:S(2)}) copy-start(f32[48,2048]{1,0:T(8,128)} %get-tuple-element.38) | copy-start | bytes 1179652

commit v3 on v2

--- a/solution.py
+++ b/solution.py
@@ -55,6 +55,12 @@
 
 def hot_bf16(mask):
     return jnp.where(mask, 1.0, 0.0).astype(BF16)
+
+
+def identity(size):
+    first = lax.broadcasted_iota(jnp.int32, (size, size), 0)
+    second = lax.broadcasted_iota(jnp.int32, (size, size), 1)
+    return jnp.where(first == second, 1.0, 0.0)
 
 
 def sigmoid(value):
@@ -125,8 +131,7 @@
     capacity,
     ray_ref,
     sam_ref,
-    cell_ref,
-    live_ref,
+    counts_ref,
     pos_ref,
     codes_ref,
     table_ref,
@@ -173,6 +178,10 @@
     shift_ref,
     rows_ref,
     sums_ref,
+    freqcol_ref,
+    b1col_ref,
+    b2col_ref,
+    hot_ref,
     send_sems,
     recv_sems,
 ):
@@ -200,18 +209,13 @@
     chunk = chunk_of(slots, 1024)
     steps = slots // chunk
 
-    parts = split3(pos_ref[...].reshape(3 * samples, rays))
-    code_hot = hot_bf16(one_hot(codes_ref[...], codes_total))
-    table_parts = split3(table_ref[...])
-    app_ref[...] = (nn(table_parts[2], code_hot) + nn(table_parts[1], code_hot)) + nn(
-        table_parts[0], code_hot
-    )
+    parts = jnp.concatenate(split3(pos_ref[...].reshape(3 * samples, rays)), axis=1)
 
     def pick_rows(step, carry):
         here = pl.ds(pl.multiple_of(step * chunk, 128), chunk)
         ray_hot = hot_bf16(one_hot(ray_ref[:, here], rays))
         sam_hot = one_hot(sam_ref[:, here], samples)
-        picked = (nn(parts[2], ray_hot) + nn(parts[1], ray_hot)) + nn(parts[0], ray_hot)
+        picked = nn(parts, jnp.concatenate([ray_hot] * 3, axis=0))
         for axis in range(3):
             part = picked[axis * samples : (axis + 1) * samples]
             slot_ref[axis : axis + 1, here] = jnp.sum(
@@ -229,6 +233,35 @@
     start_all(*extra_args)
     pos_land[me] = pos_send[me]
     extra_land[me] = extra_ref[...]
+
+    freqcol_ref[...] = tn(freq_ref[...], identity(3), HIGH)
+    for bias_ref, column_ref in ((b1_ref, b1col_ref), (b2_ref, b2col_ref)):
+        columns = tn(bias_ref[...], identity(cell_dev), HIGH)
+        for j in range(cell_dev):
+            column_ref[j] = columns[:, j : j + 1]
+    code_hot = hot_bf16(one_hot(codes_ref[...], codes_total))
+    table_parts = split3(table_ref[...])
+    app_ref[...] = (nn(table_parts[2], code_hot) + nn(table_parts[1], code_hot)) + nn(
+        table_parts[0], code_hot
+    )
+    for ref in (gw1_ref, gb1_ref, gw2_ref, gb2_ref, gh_ref, term_send):
+        ref[...] = jnp.zeros_like(ref)
+    code_row = 3 * cell_dev
+
+    def codes_of_all():
+        return jnp.concatenate(
+            [extra_land[n][code_row : code_row + 1, :rays] for n in range(owners)], axis=1
+        ).astype(jnp.int32)
+
+    block = chunk_of(codes_total, 512)
+    kept_hot = hot_ref.shape[0] == codes_total
+    if kept_hot:
+        wait_all(*extra_args)
+        all_codes = codes_of_all()
+        for first_code in range(0, codes_total, block):
+            hot_ref[first_code : first_code + block, :] = hot_bf16(
+                one_hot(all_codes - first_code, block)
+            )
     wait_all(*pos_args)
     for j in range(cell_dev):
         cellpos_ref[j] = jnp.concatenate(
@@ -242,15 +275,15 @@
     def forward(step, carry):
         j = step // blocks
         here = pl.ds(pl.multiple_of((step % blocks) * lanes, 128), lanes)
-        encoded = encode_block(cellpos_ref[j, :, here], freq_ref[...])
+        encoded = encode_block(cellpos_ref[j, :, here], freqcol_ref[...])
         enc_ref[j, :, here] = encoded
-        pre = tn(w1_ref[j], encoded) + b1_ref[j]
+        pre = tn(w1_ref[j], encoded) + b1col_ref[j]
         sig = sigmoid(pre)
         act = pre * sig
         d1_ref[j, :, here] = sig + act * (1.0 - sig)
         act = act.astype(BF16)
         act1_ref[j, :, here] = act
-        pre = tn(w2_ref[j], act) + b2_ref[j]
+        pre = tn(w2_ref[j], act) + b2col_ref[j]
         sig = sigmoid(pre)
         act = pre * sig
         d2_ref[j, :, here] = sig + act * (1.0 - sig)
@@ -269,7 +302,8 @@
     start_all(*out_args)
     out_land[me] = out_send[me]
 
-    wait_all(*extra_args)
+    if not kept_hot:
+        wait_all(*extra_args)
 
     def place_heads(n, carry):
         for k in range(3):
@@ -281,25 +315,32 @@
     lax.fori_loop(0, owners, place_heads, 0)
     shift_ref[...] = nn(heads_ref[...], app_ref[...], HIGH)
     rows_ref[...] = jnp.zeros_like(rows_ref)
-    shift_parts = split3(shift_ref[...])
+    shift_parts = jnp.concatenate(split3(shift_ref[...]), axis=1)
     wait_all(*out_args)
     for n in range(owners):
         outs_ref[:, n * per_owner : (n + 1) * per_owner] = out_land[n]
+
+    counts_col = tn(counts_ref[...].astype(F32), jnp.ones((1, 1), F32), HIGH)
+    counts_col = jnp.round(counts_col).astype(jnp.int32)
+
+    def slot_places(step, size):
+        first_slot = lax.broadcasted_iota(jnp.int32, (cells, size), 0) * capacity
+        return first_slot, lax.broadcasted_iota(jnp.int32, (cells, size), 1) + step * size
 
     def gather_rows(step, carry):
         here = pl.ds(pl.multiple_of(step * chunk, 128), chunk)
         ray_hot = hot_bf16(one_hot(ray_ref[:, here], rays))
         sam_hot = one_hot(sam_ref[:, here], samples)
-        cell_hot = one_hot(cell_ref[:, here], cells)
-        shifts = (nn(shift_parts[2], ray_hot) + nn(shift_parts[1], ray_hot)) + nn(
-            shift_parts[0], ray_hot
-        )
+        first_slot, slot_id = slot_places(step, chunk)
+        cell_hot = (slot_id >= first_slot) & (slot_id < first_slot + capacity)
+        shifts = nn(shift_parts, jnp.concatenate([ray_hot] * 3, axis=0))
         columns = [outs_ref[0:1, here]]
         for k in range(3):
             part = shifts[k * cells : (k + 1) * cells]
             picked = jnp.sum(jnp.where(cell_hot, part, 0.0), axis=0, keepdims=True)
             columns.append(outs_ref[k + 1 : k + 2, here] + picked)
-        columns.append(live_ref[:, here])
+        live = (slot_id >= first_slot) & (slot_id < first_slot + counts_col)
+        columns.append(jnp.sum(jnp.where(live, 1.0, 0.0), axis=0, keepdims=True))
         spread = [jnp.where(sam_hot, column, 0.0).astype(BF16) for column in columns]
         rows_ref[...] += nt(jnp.concatenate(spread, axis=0), ray_hot)
         return carry
@@ -341,7 +382,8 @@
         here = pl.ds(pl.multiple_of(step * chunk, 128), chunk)
         ray_hot = hot_bf16(one_hot(ray_ref[:, here], rays))
         sam_hot = one_hot(sam_ref[:, here], samples)
-        cell_hot = one_hot(cell_ref[:, here], cells)
+        first_slot, slot_id = slot_places(step, chunk)
+        cell_hot = (slot_id >= first_slot) & (slot_id < first_slot + capacity)
         picked = nn(stacked, ray_hot)
         spread = []
         for k in range(4):
@@ -378,7 +420,6 @@
             ] = partial_ref[pl.ds(k * cells + n * cell_dev, cell_dev), :]
         return carry
 
-    term_send[...] = jnp.zeros_like(term_send)
     lax.fori_loop(0, owners, place_terms, 0)
     term_args = (
         me,
@@ -396,9 +437,6 @@
             [slope_land[n][:, j * capacity : (j + 1) * capacity] for n in range(owners)], axis=1
         )
 
-    for ref in (gw1_ref, gb1_ref, gw2_ref, gb2_ref, gh_ref):
-        ref[...] = jnp.zeros_like(ref)
-
     def backward(step, carry):
         j = step // blocks
         here = pl.ds(pl.multiple_of((step % blocks) * lanes, 128), lanes)
@@ -407,10 +445,10 @@
         gh_ref[j] += nt(slopes, act2_ref[j, :, here])
         delta = (tn(head_ref[j], slopes) * d2_ref[j, :, here]).astype(BF16)
         gw2_ref[j] += nt(act1_ref[j, :, here], delta)
-        gb2_ref[j] += nt(ones, delta)[0:1]
+        gb2_ref[pl.ds(j, 1), :] += nt(ones, delta)[0:1]
         delta = (nn(w2_ref[j], delta) * d1_ref[j, :, here]).astype(BF16)
         gw1_ref[j] += nt(enc_ref[j, :, here], delta)
-        gb1_ref[j] += nt(ones, delta)[0:1]
+        gb1_ref[pl.ds(j, 1), :] += nt(ones, delta)[0:1]
         return carry
 
     lax.fori_loop(0, cell_dev * blocks, backward, 0)
@@ -419,19 +457,23 @@
     total = term_land[0]
     for n in range(1, owners):
         total = total + term_land[n]
-    ga_ref[...] = total[app_width:, :app_width]
+    for j in range(cell_dev):
+        for k in range(3):
+            row = app_width + k * cell_dev + j
+            ga_ref[j, k : k + 1, :] = total[row : row + 1, :app_width]
     terms = jnp.concatenate([term_land[n][:app_width, :rays] for n in range(owners)], axis=1)
-    code_row = 3 * cell_dev
-    all_codes = jnp.concatenate(
-        [extra_land[n][code_row : code_row + 1, :rays] for n in range(owners)], axis=1
-    ).astype(jnp.int32)
-    term_parts = split3(terms)
-    block = chunk_of(codes_total, 512)
+    term_parts = jnp.concatenate(split3(terms), axis=0)
+    if not kept_hot:
+        all_codes = codes_of_all()
     for first_code in range(0, codes_total, block):
-        hot = hot_bf16(one_hot(all_codes - first_code, block))
+        if kept_hot:
+            hot = hot_ref[first_code : first_code + block, :]
+        else:
+            hot = hot_bf16(one_hot(all_codes - first_code, block))
+        sums = nt(term_parts, hot)
         gt_ref[:, first_code : first_code + block] = (
-            nt(term_parts[2], hot) + nt(term_parts[1], hot)
-        ) + nt(term_parts[0], hot)
+            sums[2 * app_width :] + sums[app_width : 2 * app_width]
+        ) + sums[:app_width]
 
 
 def local(
@@ -463,9 +505,6 @@
     listed = dispatch.reshape(1, rows_local)
     slot_ray = listed // samples
     slot_sam = listed - slot_ray * samples
-    slot_cell = lax.broadcasted_iota(jnp.int32, (lists, capacity), 0).reshape(1, rows_local)
-    live = (jnp.arange(capacity, dtype=jnp.int32)[None, :] < counts[:, None]).astype(F32)
-    live = live.reshape(1, rows_local)
     pos_grid = jnp.transpose(positions.reshape(3, rays, samples), (0, 2, 1))
     delta_grid = deltas.reshape(rays, samples).T
 
@@ -480,14 +519,15 @@
         axis=0,
     )
     term_rows = app_width + 3 * cell_dev
+    hot_rows = codes_total if owners * rays <= 2048 else 16
     in_vmem = pl.BlockSpec(memory_space=pltpu.VMEM)
     outs = (
         jax.ShapeDtypeStruct((cell_dev, encoding, width), F32),
-        jax.ShapeDtypeStruct((cell_dev, 1, width), F32),
+        jax.ShapeDtypeStruct((cell_dev, width), F32),
         jax.ShapeDtypeStruct((cell_dev, width, width), F32),
-        jax.ShapeDtypeStruct((cell_dev, 1, width), F32),
+        jax.ShapeDtypeStruct((cell_dev, width), F32),
         jax.ShapeDtypeStruct((cell_dev, 4, width), F32),
-        jax.ShapeDtypeStruct((3 * cell_dev, app_width), F32),
+        jax.ShapeDtypeStruct((cell_dev, 3, app_width), F32),
         jax.ShapeDtypeStruct((app_width, codes_total), F32),
     )
     (
@@ -501,7 +541,7 @@
     ) = pl.pallas_call(
         functools.partial(whole_kernel, owners, capacity),
         out_shape=outs,
-        in_specs=[in_vmem] * 17,
+        in_specs=[in_vmem] * 16,
         out_specs=(in_vmem,) * 7,
         scratch_shapes=[
             pltpu.VMEM((owners,) + extra.shape, F32),
@@ -530,6 +570,10 @@
             pltpu.VMEM((3 * lists, rays), F32),
             pltpu.VMEM((5 * samples, rays), F32),
             pltpu.VMEM((3 * lists, rays), F32),
+            pltpu.VMEM((frequencies.shape[1], 3), F32),
+            pltpu.VMEM((cell_dev, width, 1), F32),
+            pltpu.VMEM((cell_dev, width, 1), F32),
+            pltpu.VMEM((hot_rows, owners * rays), BF16),
             pltpu.SemaphoreType.DMA((5, owners)),
             pltpu.SemaphoreType.DMA((5, owners)),
         ],
@@ -540,28 +584,26 @@
     )(
         slot_ray,
         slot_sam,
-        slot_cell,
-        live,
+        counts.reshape(1, lists),
         pos_grid,
         ray_codes.reshape(1, rays),
         app_table,
         extra,
-        frequencies.T,
+        frequencies,
         w_first,
-        b_first[:, :, None],
+        b_first,
         w_second,
-        b_second[:, :, None],
+        b_second,
         head_out,
         delta_grid,
         background,
         target,
     )
-    grad_head_app = jnp.transpose(grad_head_app.reshape(3, cell_dev, app_width), (1, 0, 2))
     return (
         grad_w_first,
-        grad_b_first.reshape(cell_dev, width),
+        grad_b_first,
         grad_w_second,
-        grad_b_second.reshape(cell_dev, width),
+        grad_b_second,
         grad_head_out,
         grad_head_app,
         grad_table,

time: 70.7 us -> 65 us (0.919)
  local copies, waits for them, and re-layouts: 13.5 us -> 9.55 us
  Pallas kernels: 54.8 us -> 53 us
    reshape x2 -> x0, local copies, waits for them, and re-layouts: 2.01 us -> none  [the longest x1 1.32 us: local(): grad_head_app.reshape(3, cell_dev, app_width)]
    pallas_call x1, Pallas kernels: 54.8 us -> 53 us  [local(): pl.pallas_call(functools.partial(whole_kernel, owners, capacity), out_sha...]
    broadcast_in_dim x2 -> x0, local copies, waits for them, and re-layouts: 1.72 us -> none  [the longest x1 0.86 us: local(): b_first[:, :, None]]
    pallas_call x0 -> x1, local copies, waits for them, and re-layouts: none -> 1.32 us  [local(): pl.pallas_call(functools.partial(whole_kernel, owners, capacity), out_sha...]
    unnamed x28 -> x24, local copies, waits for them, and re-layouts: 6.5 us -> 5.67 us
where the time goes in v3:
time: 65 us; the launch traced here: 64.6 us
  Pallas kernels  53 us (82%)
  local copies, waits for them, and re-layouts  9.55 us (15%)
  other arithmetic  1.37 us (2%)
  between operations  0.69 us (1%)
    pallas_call x1, Pallas kernels, local(): pl.pallas_call(functools.partial(whole_kernel, owners, capacity), out_sha...  53 us
    unnamed x24, local copies, waits for them, and re-layouts  5.67 us
    pallas_call x1, local copies, waits for them, and re-layouts, local(): pl.pallas_call(functools.partial(whole_kernel, owners, capacity), out_sha...  1.32 us

profile of v3, /device:TPU:13, one launch (start us, length us, event | category | flops | bytes accessed | tf_op | source)
XLA Modules:
  0.0 64.6 jit_solution(4693655202571954778)
XLA Ops:
  0.6 0.0 copy-start.8
  0.6 0.0 copy-start.7
  0.7 0.6 copy-done.8
  1.3 0.0 copy-done.7
  1.4 0.6 pad_maximum_fusion.extra_ref
  2.0 0.0 copy-start.3
  2.0 0.9 %reshape.117 = s32[1,6144]{1,0:T(1,128)S(1)} reshape(s32[32,192]{1,0:T(8,128)} %param.28) | data formatting | bytes 49152 | tf_op jit(solution)/shard_map/reshape | solution.py:505
  2.8 0.0 copy-start.2
  2.8 0.8 %multiply_subtract_fusion = (s32[1,6144]{1,0:T(1,128)}, s32[1,6144]{1,0:T(1,128)}) fusion(s32[1,6144]{1,0:T(1,128)S(1)} %reshape.117), kind=kLoop, calls=%fused_computation.1 | loop fusion | flops 61440 | bytes 73728 | tf_op jit(solution)/shard_map/sub | solution.py:507
  3.6 0.0 copy-done.3
  3.6 0.1 reshape.122
  3.7 0.7 %copy.24 = f32[64,96]{0,1:T(8,128)} copy(f32[64,96]{1,0:T(8,128)S(1)} %reshape.122) | data formatting | bytes 49152 | tf_op jit(solution)/shard_map/reshape | solution.py:509
  4.4 0.0 copy-done.2
  4.4 0.1 reshape.119
  4.5 0.8 %copy.23 = f32[3,64,96]{1,2,0:T(8,128)} copy(f32[3,64,96]{2,1,0:T(8,128)S(1)} %reshape.119) | data formatting | bytes 147456 | tf_op jit(solution)/shard_map/reshape | solution.py:508
  5.3 53.0 %whole.1 = (f32[2,128,256]{2,1,0:T(8,128)}, f32[2,256]{1,0:T(2,128)}, f32[2,256,256]{2,1,0:T(8,128)}, f32[2,256]{1,0:T(2,128)}, f32[2,4,256]{2,1,0:T(4,128)}, /*index=5*/f32[2,3,48]{2,1,0:T(4,128)}, f32[48,2048]{1,0:T(8,128)}) custom-call(s32[1,6144]{1,0:T(1,128)} %get-tuple-element.22.ray_ref, s32[1,6144]{1,0:T(1,128)} %get-tuple-element.21.sam_ref, ...), custom_call_target="tpu_custom_call" | custom-call | tf_op jit(solution)/shard_map/whole/pallas_call | solution.py:541
  58.3 0.0 copy-start
  58.3 1.3 %copy.25 = f32[2,3,48]{2,0,1:T(2,128)} copy(f32[2,3,48]{2,1,0:T(4,128)} %get-tuple-element.19) | data formatting | bytes 2304 | tf_op jit(solution)/shard_map/whole/pallas_call | solution.py:541
  59.6 0.0 copy-start.6
  59.6 1.7 %copy.32 = f32[2,128,256]{2,1,0:T(8,128)} copy(f32[2,128,256]{2,1,0:T(8,128)} %get-tuple-element.30) | data formatting | bytes 524288
  61.3 0.0 copy-done.6
  61.3 0.6 copy.33
  61.9 0.0 copy-done
  61.9 0.0 copy-start.5
  61.9 0.0 copy-start.4
  61.9 0.0 copy-start.1
  61.9 0.8 %copy.34 = f32[2,256,256]{2,1,0:T(8,128)} copy(f32[2,256,256]{2,1,0:T(8,128)S(1)} %copy-done) | data formatting | bytes 1048576
  62.7 0.0 copy-done.5
  62.7 0.6 copy.35
  63.3 0.0 copy-done.4
  63.3 0.6 copy.36
  63.9 0.0 copy-done.1
  63.9 0.7 %copy.37 = f32[48,2048]{1,0:T(8,128)} copy(f32[48,2048]{1,0:T(8,128)S(1)} %copy-done.1) | data formatting | bytes 786432
  (3 shorter events, 0.0 us)
Async XLA Ops:
  0.6 0.7 %copy-start.8 = (s32[64]{0:T(128)S(1)}, s32[64]{0:T(128)}, u32[]{:S(2)}) copy-start(s32[64]{0:T(128)} %param.19) | copy-start | bytes 772
  0.6 0.7 %copy-start.7 = (bf16[2,3,48]{2,0,1:T(2,128)(2,1)S(1)}, bf16[2,3,48]{2,0,1:T(2,128)(2,1)}, u32[]{:S(2)}) copy-start(bf16[2,3,48]{2,0,1:T(2,128)(2,1)} %param.26) | copy-start | bytes 1732
  2.0 1.6 %copy-start.3 = (f32[6144]{0:T(1024)S(1)}, f32[6144]{0:T(1024)}, u32[]{:S(2)}) copy-start(f32[6144]{0:T(1024)} %param.16) | copy-start | bytes 73732
  2.8 1.6 %copy-start.2 = (f32[3,6144]{1,0:T(4,128)S(1)}, f32[3,6144]{1,0:T(4,128)}, u32[]{:S(2)}) copy-start(f32[3,6144]{1,0:T(4,128)} %param.15) | copy-start | bytes 221188
  58.3 3.6 %copy-start = (f32[2,256,256]{2,1,0:T(8,128)S(1)}, f32[2,256,256]{2,1,0:T(8,128)}, u32[]{:S(2)}) copy-start(f32[2,256,256]{2,1,0:T(8,128)} %get-tuple-element.32) | copy-start | bytes 1572868
  59.6 1.7 %copy-start.6 = (f32[2,256]{1,0:T(2,128)S(1)}, f32[2,256]{1,0:T(2,128)}, u32[]{:S(2)}) copy-start(f32[2,256]{1,0:T(2,128)} %get-tuple-element.31) | copy-start | bytes 6148
  61.9 0.8 %copy-start.5 = (f32[2,256]{1,0:T(2,128)S(1)}, f32[2,256]{1,0:T(2,128)}, u32[]{:S(2)}) copy-start(f32[2,256]{1,0:T(2,128)} %get-tuple-element.33) | copy-start | bytes 6148
  61.9 1.4 %copy-start.4 = (f32[2,4,256]{2,1,0:T(4,128)S(1)}, f32[2,4,256]{2,1,0:T(4,128)}, u32[]{:S(2)}) copy-start(f32[2,4,256]{2,1,0:T(4,128)} %get-tuple-element.34) | copy-start | bytes 24580
  61.9 2.0 %copy-start.1 = (f32[48,2048]{1,0:T(8,128)S(1)}, f32[48,2048]{1,0:T(8,128)}, u32[]{:S(2)}) copy-start(f32[48,2048]{1,0:T(8,128)} %get-tuple-element.36) | copy-start | bytes 1179652

commit v4 on v3

--- a/solution.py
+++ b/solution.py
@@ -55,6 +55,17 @@
 
 def hot_bf16(mask):
     return jnp.where(mask, 1.0, 0.0).astype(BF16)
+
+
+def in_pairs(steps, body):
+    width = 2 if steps % 2 == 0 else 1
+
+    def several(step, carry):
+        for part in range(width):
+            carry = body(step * width + part, carry)
+        return carry
+
+    lax.fori_loop(0, steps // width, several, 0)
 
 
 def identity(size):
@@ -223,7 +234,7 @@
             )
         return carry
 
-    lax.fori_loop(0, steps, pick_rows, 0)
+    in_pairs(steps, pick_rows)
     for n in range(owners):
         pos_send[n] = slot_ref[:, n * per_owner : (n + 1) * per_owner]
     pl.semaphore_wait(barrier, owners - 1)
@@ -292,7 +303,7 @@
         cellout_ref[j, :, here] = nn(head_ref[j], act)
         return carry
 
-    lax.fori_loop(0, cell_dev * blocks, forward, 0)
+    in_pairs(cell_dev * blocks, forward)
     outs = [cellout_ref[j] for j in range(cell_dev)]
     for n in range(owners):
         out_send[n] = jnp.concatenate(
@@ -345,7 +356,7 @@
         rows_ref[...] += nt(jnp.concatenate(spread, axis=0), ray_hot)
         return carry
 
-    lax.fori_loop(0, steps, gather_rows, 0)
+    in_pairs(steps, gather_rows)
     raw = [rows_ref[k * samples : (k + 1) * samples] for k in range(4)]
     routed = rows_ref[4 * samples : 5 * samples]
     deltas = deltas_ref[...]
@@ -395,7 +406,7 @@
         sums_ref[...] += nt(jnp.concatenate(spread, axis=0), ray_hot)
         return carry
 
-    lax.fori_loop(0, steps, spread_slopes, 0)
+    in_pairs(steps, spread_slopes)
     for n in range(owners):
         slope_send[n] = slope_ref[:, n * per_owner : (n + 1) * per_owner]
     slope_args = (
@@ -451,7 +462,7 @@
         gb1_ref[pl.ds(j, 1), :] += nt(ones, delta)[0:1]
         return carry
 
-    lax.fori_loop(0, cell_dev * blocks, backward, 0)
+    in_pairs(cell_dev * blocks, backward)
 
     wait_all(*term_args)
     total = term_land[0]

time: 65 us -> 63.6 us (0.978)
  Pallas kernels: 53 us -> 51.6 us
    pallas_call x1, Pallas kernels: 53 us -> 51.6 us  [local(): pl.pallas_call(functools.partial(whole_kernel, owners, capacity), out_sha...]
where the time goes in v4:
time: 63.6 us; the launch traced here: 63.2 us
  Pallas kernels  51.6 us (81%)
  local copies, waits for them, and re-layouts  9.55 us (15%)
  other arithmetic  1.37 us (2%)
  between operations  0.69 us (1%)
    pallas_call x1, Pallas kernels, local(): pl.pallas_call(functools.partial(whole_kernel, owners, capacity), out_sha...  51.6 us
    unnamed x24, local copies, waits for them, and re-layouts  5.67 us
    pallas_call x1, local copies, waits for them, and re-layouts, local(): pl.pallas_call(functools.partial(whole_kernel, owners, capacity), out_sha...  1.32 us

profile of v4, /device:TPU:13, one launch (start us, length us, event | category | flops | bytes accessed | tf_op | source)
XLA Modules:
  0.0 63.2 jit_solution(7832019143891401614)
XLA Ops:
  0.6 0.0 copy-start.8
  0.6 0.0 copy-start.7
  0.7 0.6 %copy-done.8 = s32[64]{0:T(128)S(1)} copy-done((s32[64]{0:T(128)S(1)}, s32[64]{0:T(128)}, u32[]{:S(2)}) %copy-start.8) | copy-done | bytes 280
  1.3 0.0 copy-done.7
  1.4 0.6 pad_maximum_fusion.extra_ref
  2.0 0.0 copy-start.3
  2.0 0.9 %reshape.117 = s32[1,6144]{1,0:T(1,128)S(1)} reshape(s32[32,192]{1,0:T(8,128)} %param.28) | data formatting | bytes 49152 | tf_op jit(solution)/shard_map/reshape | solution.py:516
  2.8 0.0 copy-start.2
  2.8 0.8 %multiply_subtract_fusion = (s32[1,6144]{1,0:T(1,128)}, s32[1,6144]{1,0:T(1,128)}) fusion(s32[1,6144]{1,0:T(1,128)S(1)} %reshape.117), kind=kLoop, calls=%fused_computation.1 | loop fusion | flops 61440 | bytes 73728 | tf_op jit(solution)/shard_map/sub | solution.py:518
  3.6 0.0 copy-done.3
  3.6 0.1 reshape.122
  3.7 0.7 %copy.24 = f32[64,96]{0,1:T(8,128)} copy(f32[64,96]{1,0:T(8,128)S(1)} %reshape.122) | data formatting | bytes 49152 | tf_op jit(solution)/shard_map/reshape | solution.py:520
  4.4 0.0 copy-done.2
  4.4 0.1 reshape.119
  4.5 0.8 %copy.23 = f32[3,64,96]{1,2,0:T(8,128)} copy(f32[3,64,96]{2,1,0:T(8,128)S(1)} %reshape.119) | data formatting | bytes 147456 | tf_op jit(solution)/shard_map/reshape | solution.py:519
  5.3 51.6 %whole.1 = (f32[2,128,256]{2,1,0:T(8,128)}, f32[2,256]{1,0:T(2,128)}, f32[2,256,256]{2,1,0:T(8,128)}, f32[2,256]{1,0:T(2,128)}, f32[2,4,256]{2,1,0:T(4,128)}, /*index=5*/f32[2,3,48]{2,1,0:T(4,128)}, f32[48,2048]{1,0:T(8,128)}) custom-call(s32[1,6144]{1,0:T(1,128)} %get-tuple-element.22.ray_ref, s32[1,6144]{1,0:T(1,128)} %get-tuple-element.21.sam_ref, ...), custom_call_target="tpu_custom_call" | custom-call | tf_op jit(solution)/shard_map/whole/pallas_call | solution.py:552
  56.9 0.0 copy-start
  56.9 1.3 %copy.25 = f32[2,3,48]{2,0,1:T(2,128)} copy(f32[2,3,48]{2,1,0:T(4,128)} %get-tuple-element.19) | data formatting | bytes 2304 | tf_op jit(solution)/shard_map/whole/pallas_call | solution.py:552
  58.2 0.0 copy-start.6
  58.2 1.7 %copy.32 = f32[2,128,256]{2,1,0:T(8,128)} copy(f32[2,128,256]{2,1,0:T(8,128)} %get-tuple-element.30) | data formatting | bytes 524288
  59.9 0.0 copy-done.6
  59.9 0.6 copy.33
  60.4 0.0 copy-done
  60.4 0.0 copy-start.5
  60.4 0.0 copy-start.4
  60.4 0.0 copy-start.1
  60.5 0.8 %copy.34 = f32[2,256,256]{2,1,0:T(8,128)} copy(f32[2,256,256]{2,1,0:T(8,128)S(1)} %copy-done) | data formatting | bytes 1048576
  61.2 0.0 copy-done.5
  61.2 0.6 copy.35
  61.8 0.0 copy-done.4
  61.8 0.6 copy.36
  62.4 0.0 copy-done.1
  62.4 0.7 %copy.37 = f32[48,2048]{1,0:T(8,128)} copy(f32[48,2048]{1,0:T(8,128)S(1)} %copy-done.1) | data formatting | bytes 786432
  (3 shorter events, 0.0 us)
Async XLA Ops:
  0.6 0.7 %copy-start.8 = (s32[64]{0:T(128)S(1)}, s32[64]{0:T(128)}, u32[]{:S(2)}) copy-start(s32[64]{0:T(128)} %param.19) | copy-start | bytes 772
  0.6 0.7 %copy-start.7 = (bf16[2,3,48]{2,0,1:T(2,128)(2,1)S(1)}, bf16[2,3,48]{2,0,1:T(2,128)(2,1)}, u32[]{:S(2)}) copy-start(bf16[2,3,48]{2,0,1:T(2,128)(2,1)} %param.26) | copy-start | bytes 1732
  2.0 1.6 %copy-start.3 = (f32[6144]{0:T(1024)S(1)}, f32[6144]{0:T(1024)}, u32[]{:S(2)}) copy-start(f32[6144]{0:T(1024)} %param.16) | copy-start | bytes 73732
  2.8 1.6 %copy-start.2 = (f32[3,6144]{1,0:T(4,128)S(1)}, f32[3,6144]{1,0:T(4,128)}, u32[]{:S(2)}) copy-start(f32[3,6144]{1,0:T(4,128)} %param.15) | copy-start | bytes 221188
  56.9 3.6 %copy-start = (f32[2,256,256]{2,1,0:T(8,128)S(1)}, f32[2,256,256]{2,1,0:T(8,128)}, u32[]{:S(2)}) copy-start(f32[2,256,256]{2,1,0:T(8,128)} %get-tuple-element.32) | copy-start | bytes 1572868
  58.2 1.7 %copy-start.6 = (f32[2,256]{1,0:T(2,128)S(1)}, f32[2,256]{1,0:T(2,128)}, u32[]{:S(2)}) copy-start(f32[2,256]{1,0:T(2,128)} %get-tuple-element.31) | copy-start | bytes 6148
  60.4 0.8 %copy-start.5 = (f32[2,256]{1,0:T(2,128)S(1)}, f32[2,256]{1,0:T(2,128)}, u32[]{:S(2)}) copy-start(f32[2,256]{1,0:T(2,128)} %get-tuple-element.33) | copy-start | bytes 6148
  60.4 1.4 %copy-start.4 = (f32[2,4,256]{2,1,0:T(4,128)S(1)}, f32[2,4,256]{2,1,0:T(4,128)}, u32[]{:S(2)}) copy-start(f32[2,4,256]{2,1,0:T(4,128)} %get-tuple-element.34) | copy-start | bytes 24580
  60.4 2.0 %copy-start.1 = (f32[48,2048]{1,0:T(8,128)S(1)}, f32[48,2048]{1,0:T(8,128)}, u32[]{:S(2)}) copy-start(f32[48,2048]{1,0:T(8,128)} %get-tuple-element.36) | copy-start | bytes 1179652
